TPU v7x, 512 devices: a whole 4x4x16 slice. The times are simulated.
512 devices in a mesh: ctx: 32 (over y, z_hi, core), resp: 16 (over z_lo, x).
Axes of the slice: x: 4, y: 4, z: 16 (z_hi: 4, z_lo: 4; z = z_hi * 4 + z_lo), core: 2. Of those that a mesh axis runs over, the one named last changes fastest.
Arguments:
- queries: bfloat16 [32, 2048, 1024], P('ctx', 'resp'), may hold values from -4.5 to 4.5
- resp_keys: bfloat16 [32, 2048, 128], P('ctx', 'resp'), may hold values from -4.5 to 4.5
- resp_values: bfloat16 [32, 2048, 128], P('ctx', 'resp'), may hold values from -6 to 6
- prompt_keys: bfloat16 [2048, 128], P('ctx'), may hold values from -4.5 to 4.5
- prompt_values: bfloat16 [2048, 128], P('ctx'), may hold values from -6 to 6
- cotangent: bfloat16 [32, 2048, 1024], P('ctx', 'resp'), may hold values from -6 to 6
- lengths: int32 [32], P('ctx'), may hold values from 256 to 2048, as said below
Outputs:
- attn_out: bfloat16 [32, 2048, 1024], P('ctx', 'resp')
- grad_queries: bfloat16 [32, 2048, 1024], P('ctx', 'resp')
- grad_resp_keys: float32 [32, 2048, 128], P('ctx', 'resp')
- grad_resp_values: float32 [32, 2048, 128], P('ctx', 'resp')
- grad_prompt_keys: float32 [2048, 128], P('ctx')
- grad_prompt_values: float32 [2048, 128], P('ctx')
Inputs may be any that keep to these rules, and one draw needn't show every extreme that they name: `lengths`: some response has length 2048 in every draw.
All inputs are finite; a program needn't handle non-finite values.
Results may differ from a plain program's by a relative error of at most 0.0098.
Values may be sent and summed in bfloat16 or wider, within the bound.
No kernel may reach another device: no remote copies, remote signals or barrier semaphores. Data moves between devices by JAX's collectives and lax.ppermute only.
A program may use at most 64 MiB of HBM per device.

v0:
```python
import math

import jax
import jax.numpy as jnp
from jax import lax
from jax.sharding import PartitionSpec as P


def attend_segment(rows, cot, first, length, pkeys, pvalues, rkeys, rvalues, buffers, block_rows):
    positions = rows.shape[0]
    width = rows.shape[1]
    head_size = pkeys.shape[1]
    heads = width // head_size
    count = positions * heads
    scale = 1.0 / math.sqrt(head_size)
    query_rows = rows.reshape(count, head_size)
    query_pos = first + lax.broadcasted_iota(jnp.int32, (positions, heads), 0).reshape(count)
    valid = (query_pos < length)[:, None]
    cot_rows = jnp.where(valid, cot.reshape(count, head_size), jnp.zeros((), jnp.bfloat16))
    last_key = jnp.minimum(first + positions - 1, length - 1)
    block_count = last_key // block_rows + 1
    prompt_total = pkeys.shape[0]
    prompt_block = min(prompt_total, 1024)
    prompt_steps = prompt_total // prompt_block

    def scores_of(keys, key_pos):
        raw = jnp.einsum("rd,kd->rk", query_rows, keys, preferred_element_type=jnp.float32) * scale
        if key_pos is None:
            return raw
        return jnp.where(key_pos[None, :] <= query_pos[:, None], raw, -1e30)

    def resp_piece(index):
        start = index * block_rows
        keys = lax.dynamic_slice_in_dim(rkeys, start, block_rows, 0)
        values = lax.dynamic_slice_in_dim(rvalues, start, block_rows, 0)
        key_pos = start + lax.broadcasted_iota(jnp.int32, (block_rows,), 0)
        return (keys, values, key_pos)

    def run(buffers):

        def stat_step(state, keys, key_pos):
            run_max, run_sum = state
            block = scores_of(keys, key_pos)
            new_max = jnp.maximum(run_max, jnp.max(block, 1))
            run_sum = run_sum * jnp.exp(run_max - new_max) + jnp.sum(
                jnp.exp(block - new_max[:, None]), 1
            )
            return (new_max, run_sum)

        state = (jnp.full((count,), -1e30, jnp.float32), jnp.zeros((count,), jnp.float32))
        for index in range(prompt_steps):
            start = index * prompt_block
            state = stat_step(state, pkeys[start : start + prompt_block], None)

        def stat_loop(index, state):
            keys, values, key_pos = resp_piece(index)
            return stat_step(state, keys, key_pos)

        state = lax.fori_loop(0, block_count, stat_loop, state)
        lse = state[0] + jnp.log(state[1])

        def weight_of(keys, key_pos):
            return jnp.exp(scores_of(keys, key_pos) - lse[:, None])

        def out_step(total, keys, values, key_pos):
            probs = weight_of(keys, key_pos).astype(jnp.bfloat16)
            return total + jnp.dot(probs, values, preferred_element_type=jnp.float32)

        total = jnp.zeros((count, head_size), jnp.float32)
        for index in range(prompt_steps):
            start = index * prompt_block
            total = out_step(
                total,
                pkeys[start : start + prompt_block],
                pvalues[start : start + prompt_block],
                None,
            )

        def out_loop(index, total):
            keys, values, key_pos = resp_piece(index)
            return out_step(total, keys, values, key_pos)

        total = lax.fori_loop(0, block_count, out_loop, total)
        full_out = jnp.where(valid, total, 0.0)
        delta = jnp.sum(cot_rows.astype(jnp.float32) * full_out, 1)

        def grad_step(keys, values, key_pos):
            weights = weight_of(keys, key_pos)
            probs = weights.astype(jnp.bfloat16)
            dprobs = jnp.einsum("rd,kd->rk", cot_rows, values, preferred_element_type=jnp.float32)
            dscores = (weights * (dprobs - delta[:, None]) * scale).astype(jnp.bfloat16)
            query_part = jnp.dot(dscores, keys, preferred_element_type=jnp.float32)
            key_part = jnp.einsum(
                "rk,rd->kd", dscores, query_rows, preferred_element_type=jnp.float32
            )
            value_part = jnp.einsum(
                "rk,rd->kd", probs, cot_rows, preferred_element_type=jnp.float32
            )
            return (query_part, key_part, value_part)

        prompt_kgrad, prompt_vgrad, resp_kgrad, resp_vgrad = buffers
        grad_total = jnp.zeros((count, head_size), jnp.float32)
        for index in range(prompt_steps):
            start = index * prompt_block
            query_part, key_part, value_part = grad_step(
                pkeys[start : start + prompt_block], pvalues[start : start + prompt_block], None
            )
            grad_total = grad_total + query_part
            prompt_kgrad = prompt_kgrad.at[start : start + prompt_block].add(key_part)
            prompt_vgrad = prompt_vgrad.at[start : start + prompt_block].add(value_part)

        def grad_loop(index, carry):
            grad_sum, key_grads, value_grads = carry
            keys, values, key_pos = resp_piece(index)
            start = index * block_rows
            query_part, key_part, value_part = grad_step(keys, values, key_pos)
            key_grads = lax.dynamic_update_slice_in_dim(
                key_grads,
                lax.dynamic_slice_in_dim(key_grads, start, block_rows, 0) + key_part,
                start,
                0,
            )
            value_grads = lax.dynamic_update_slice_in_dim(
                value_grads,
                lax.dynamic_slice_in_dim(value_grads, start, block_rows, 0) + value_part,
                start,
                0,
            )
            return (grad_sum + query_part, key_grads, value_grads)

        grad_total, resp_kgrad, resp_vgrad = lax.fori_loop(
            0, block_count, grad_loop, (grad_total, resp_kgrad, resp_vgrad)
        )
        out_rows = full_out.astype(jnp.bfloat16).reshape(positions, width)
        grad_rows = grad_total.astype(jnp.bfloat16).reshape(positions, width)
        return (out_rows, grad_rows, (prompt_kgrad, prompt_vgrad, resp_kgrad, resp_vgrad))

    def skip(buffers):
        empty = jnp.zeros((positions, width), jnp.bfloat16)
        return (empty, empty, buffers)

    return lax.cond(first < length, run, skip, buffers)


def per_device(queries, resp_keys, resp_values, prompt_keys, prompt_values, cotangent, lengths):
    block_rows = queries.shape[1]
    head_size = resp_keys.shape[2]
    half_rows = block_rows // 2
    resp_place = lax.axis_index("resp")
    length = lengths[0]
    all_pkeys, all_pvalues = (
        lax.all_gather(prompt_keys, "ctx", axis=0, tiled=True),
        lax.all_gather(prompt_values, "ctx", axis=0, tiled=True),
    )
    all_rkeys, all_rvalues = (
        lax.all_gather(resp_keys, "resp", axis=1, tiled=True),
        lax.all_gather(resp_values, "resp", axis=1, tiled=True),
    )
    all_rkeys = all_rkeys[0]
    all_rvalues = all_rvalues[0]
    own_rows = queries[0]
    own_cot = cotangent[0]
    own_first = resp_place * block_rows
    upper_rows = own_rows[half_rows:]
    upper_cot = own_cot[half_rows:]
    upper_first = own_first + half_rows
    prompt_total = all_pkeys.shape[0]
    resp_total = all_rkeys.shape[0]
    buffers = (
        jnp.zeros((prompt_total, head_size), jnp.float32),
        jnp.zeros((prompt_total, head_size), jnp.float32),
        jnp.zeros((resp_total, head_size), jnp.float32),
        jnp.zeros((resp_total, head_size), jnp.float32),
    )
    lower_out, lower_grad, buffers = attend_segment(
        own_rows[:half_rows],
        own_cot[:half_rows],
        own_first,
        length,
        all_pkeys,
        all_pvalues,
        all_rkeys,
        all_rvalues,
        buffers,
        block_rows,
    )
    upper_out, upper_grad, buffers = attend_segment(
        upper_rows,
        upper_cot,
        upper_first,
        length,
        all_pkeys,
        all_pvalues,
        all_rkeys,
        all_rvalues,
        buffers,
        block_rows,
    )
    attn_out = jnp.concatenate([lower_out, upper_out], 0)[None]
    grad_queries = jnp.concatenate([lower_grad, upper_grad], 0)[None]
    grad_rkeys, grad_rvalues = (
        lax.psum_scatter(buffers[2], "resp", scatter_dimension=0, tiled=True),
        lax.psum_scatter(buffers[3], "resp", scatter_dimension=0, tiled=True),
    )
    tile_keys, tile_values = (
        lax.psum_scatter(buffers[0], "ctx", scatter_dimension=0, tiled=True),
        lax.psum_scatter(buffers[1], "ctx", scatter_dimension=0, tiled=True),
    )
    grad_pkeys, grad_pvalues = lax.psum((tile_keys, tile_values), "resp")
    return (attn_out, grad_queries, grad_rkeys[None], grad_rvalues[None], grad_pkeys, grad_pvalues)


def solution(mesh):
    return jax.shard_map(
        per_device,
        mesh=mesh,
        in_specs=(
            P("ctx", "resp", None),
            P("ctx", "resp", None),
            P("ctx", "resp", None),
            P("ctx", None),
            P("ctx", None),
            P("ctx", "resp", None),
            P("ctx"),
        ),
        out_specs=(
            P("ctx", "resp", None),
            P("ctx", "resp", None),
            P("ctx", "resp", None),
            P("ctx", "resp", None),
            P("ctx", None),
            P("ctx", None),
        ),
        check_vma=False,
    )
```

profile of v0, /device:TPU:16, one launch (start us, length us, event | category | flops | bytes accessed | tf_op | source)
XLA Modules:
  0.0 1087.7 jit_solution(7257827467299638919)
XLA Ops:
  8.2 53.7 %all_gather.12 = bf16[2048,128]{1,0:T(8,128)(2,1)S(1)} all-gather(bf16[64,128]{1,0:T(8,128)(2,1)} %param.42), channel_id=1, replica_groups=mesh['ctx'=32,'resp'=16] {'ctx'}, dimensions={0}, use_global_device_ids=true | all-gather | bytes 540672 | tf_op jit(solution)/shard_map/all_gather | solution.py:152
  61.8 48.7 %all_gather.14 = bf16[2048,128]{1,0:T(8,128)(2,1)S(1)} all-gather(bf16[64,128]{1,0:T(8,128)(2,1)} %param.43), channel_id=1, replica_groups=mesh['ctx'=32,'resp'=16] {'ctx'}, dimensions={0}, use_global_device_ids=true | all-gather | bytes 540672 | tf_op jit(solution)/shard_map/all_gather | solution.py:153
  110.6 46.4 %all_gather.13 = bf16[1,2048,128]{2,1,0:T(8,128)(2,1)} all-gather(bf16[1,128,128]{2,1,0:T(8,128)(2,1)} %param.40), channel_id=1, replica_groups=mesh['ctx'=32,'resp'=16] {'resp'}, dimensions={1}, use_global_device_ids=true | all-gather | bytes 557056 | tf_op jit(solution)/shard_map/all_gather | solution.py:156
  157.0 42.1 %all_gather.15 = bf16[1,2048,128]{2,1,0:T(8,128)(2,1)} all-gather(bf16[1,128,128]{2,1,0:T(8,128)(2,1)} %param.41), channel_id=1, replica_groups=mesh['ctx'=32,'resp'=16] {'resp'}, dimensions={1}, use_global_device_ids=true | all-gather | bytes 557056 | tf_op jit(solution)/shard_map/all_gather | solution.py:157
  199.7 28.7 %conditional.2 = (bf16[64,1024]{1,0:T(8,128)(2,1)}, bf16[64,1024]{1,0:T(8,128)(2,1)}, f32[2048,128]{1,0:T(8,128)}, f32[2048,128]{1,0:T(8,128)}, f32[2048,128]{1,0:T(8,128)}, /*index=5*/f32[2048,128]{1,0:T(8,128)}) conditional(s32[]{:T(128)} %convert_element_type.98, () %tuple.88, (s32[]{:T(128)}, s32[512,1]{0,1:T(1,128)S(1)}, ...), branch_computations={%region_0.1_spmd, %region_1.15_spmd.clone} | conditional | flops 1765250944 | bytes 68465400 | solution.py:142
  204.0 2.1 fusion.83
  209.9 2.4 fusion.96
  221.4 6.2 while.130
  224.3 1.6 fusion.241
  226.0 1.7 fusion.240
  228.4 32.1 %conditional.3 = (bf16[64,1024]{1,0:T(8,128)(2,1)}, bf16[64,1024]{1,0:T(8,128)(2,1)}, f32[2048,128]{1,0:T(8,128)}, f32[2048,128]{1,0:T(8,128)}, f32[2048,128]{1,0:T(8,128)}, /*index=5*/f32[2048,128]{1,0:T(8,128)}) conditional(s32[]{:T(128)} %convert_element_type.99, (f32[2048,128]{1,0:T(8,128)}, f32[2048,128]{1,0:T(8,128)}, ...), branch_computations={%region_15.16_spmd, %region_16.30_spmd.clone} | conditional | flops 1765250944 | bytes 66368268 | solution.py:142
  235.8 2.2 fusion.108
  240.2 3.3 fusion.102
  244.2 2.3 fusion.104
  246.9 2.5 fusion.101
  250.5 2.3 fusion.103
  253.5 6.2 while.133
  258.1 1.6 fusion.221
  261.3 365.4 %reduce-scatter.9.cloned.1.call-done = f32[64,128]{1,0:T(8,128)} async-done(((f32[2048,128]{1,0:T(8,128)}), f32[64,128]{1,0:T(8,128)}) %reduce-scatter.9.cloned.1.call-update) | async-done | bytes 32784 | tf_op jit(solution)/shard_map/reduce_scatter | solution.py:206
  626.7 112.7 %reduce-scatter.11.cloned.1.call-done = f32[64,128]{1,0:T(8,128)} async-done(((f32[2048,128]{1,0:T(8,128)}), f32[64,128]{1,0:T(8,128)}) %reduce-scatter.11.cloned.1.call-update) | async-done | bytes 32784 | tf_op jit(solution)/shard_map/reduce_scatter | solution.py:207
  740.7 1.9 maximum_bitcast_fusion
  742.6 152.7 %all-reduce.3.cloned.1.call-done = (f32[64,128]{1,0:T(8,128)}, f32[64,128]{1,0:T(8,128)}) async-done(((f32[64,128]{1,0:T(8,128)}, f32[64,128]{1,0:T(8,128)}), (f32[64,128]{1,0:T(8,128)}, f32[64,128]{1,0:T(8,128)})) %all-reduce.3.cloned.1.call-update) | async-done | bytes 65552 | tf_op jit(solution)/shard_map/psum | solution.py:209
  895.3 93.1 %reduce-scatter.5.cloned.1.call-done = f32[128,128]{1,0:T(8,128)} async-done(((f32[2048,128]{1,0:T(8,128)}), f32[128,128]{1,0:T(8,128)}) %reduce-scatter.5.cloned.1.call-update) | async-done | bytes 65552 | tf_op jit(solution)/shard_map/reduce_scatter | solution.py:202
  988.3 90.1 %reduce-scatter.7.cloned.1.call-done = f32[128,128]{1,0:T(8,128)} async-done(((f32[2048,128]{1,0:T(8,128)}), f32[128,128]{1,0:T(8,128)}) %reduce-scatter.7.cloned.1.call-update) | async-done | bytes 65552 | tf_op jit(solution)/shard_map/reduce_scatter | solution.py:203
  (132 shorter events, 48.3 us)
Async XLA Ops:
  7.2 192.0 %copy-start.11 = (bf16[1,128,1024]{2,1,0:T(8,128)(2,1)S(1)}, bf16[1,128,1024]{2,1,0:T(8,128)(2,1)}, u32[]{:S(2)}) copy-start(bf16[1,128,1024]{2,1,0:T(8,128)(2,1)} %param.44) | copy-start | bytes 786436
  7.2 191.9 %copy-start.10 = (bf16[1,128,1024]{2,1,0:T(8,128)(2,1)S(1)}, bf16[1,128,1024]{2,1,0:T(8,128)(2,1)}, u32[]{:S(2)}) copy-start(bf16[1,128,1024]{2,1,0:T(8,128)(2,1)} %param.39) | copy-start | bytes 786436
  7.2 619.5 %reduce-scatter.9.cloned.1.call-start = ((), (), s32[]{:S(2)}) async-start(), calls=%async_computation.6 | async-start | bytes 1081344 | tf_op jit(solution)/shard_map/reduce_scatter | solution.py:206
  8.0 191.1 %copy-start.12 = (s32[512]{0:T(512)}, s32[512]{0:T(512)S(1)}, u32[]{:S(2)}) copy-start(s32[512]{0:T(512)S(1)} %reshape.337) | copy-start | bytes 6148
  8.2 191.0 %copy-start.13 = (s32[512,1]{0,1:T(1,128)}, s32[512,1]{0,1:T(1,128)S(1)}, u32[]{:S(2)}) copy-start(s32[512,1]{0,1:T(1,128)S(1)} %reshape.336) | copy-start | bytes 6148
  110.6 88.6 %copy-start.4 = (bf16[2048,128]{1,0:T(8,128)(2,1)}, bf16[2048,128]{1,0:T(8,128)(2,1)S(1)}, u32[]{:S(2)}) copy-start(bf16[2048,128]{1,0:T(8,128)(2,1)S(1)} %all_gather.14) | copy-start | bytes 1572868
  199.1 0.6 copy-start.14
  199.7 4.3 copy-start.5
  201.5 1.4 copy-start
  207.6 1.2 copy-start.15
  209.9 2.4 copy-start.1
  213.9 1.0 copy-start.6
  233.3 1.4 copy-start.2
  234.6 1.2 copy-start.7
  235.8 2.2 copy-start.8
  238.6 1.2 copy-start.16
  239.8 3.7 copy-start.3
  239.8 3.7 copy-start.9
  260.5 478.9 %reduce-scatter.11.cloned.1.call-start = ((), (), s32[]{:S(2)}) async-start(), calls=%async_computation.7 | async-start | bytes 1081344 | tf_op jit(solution)/shard_map/reduce_scatter | solution.py:207
  261.3 634.0 %all-reduce.3.cloned.1.call-start = ((), (), s32[]{:S(2)}) async-start(), calls=%async_computation.8 | async-start | bytes 131072 | tf_op jit(solution)/shard_map/psum | solution.py:209
  739.5 248.8 %reduce-scatter.5.cloned.1.call-start = ((), (), s32[]{:S(2)}) async-start(), calls=%async_computation.4 | async-start | bytes 1114112 | tf_op jit(solution)/shard_map/reduce_scatter | solution.py:202
  740.1 338.3 %reduce-scatter.7.cloned.1.call-start = ((), (), s32[]{:S(2)}) async-start(), calls=%async_computation.5 | async-start | bytes 1114112 | tf_op jit(solution)/shard_map/reduce_scatter | solution.py:203
Sparse Core Ops, SparseCore 0:
  260.6 366.0 reduce-scatter.8
  631.7 107.7 reduce-scatter.10
  742.5 152.7 all-reduce.2
  898.7 89.5 reduce-scatter.4
  991.6 86.7 reduce-scatter.6
where the time goes:
time: 1100 us; the launch traced here: 1090 us
  waiting for transfers between devices  816 us (74%)
  blocking collectives  191 us (17%)
  matrix products  44.8 us (4%)
  between operations  14.6 us (1%)
  local copies, waits for them, and re-layouts  11.5 us (1%)
    reduce_scatter x1, waiting for transfers between devices, per_device(): lax.psum_scatter(buffers[0], 'ctx', scatter_dimension=0, tiled=True)  365 us
    psum x1, waiting for transfers between devices, per_device(): grad_pkeys, grad_pvalues = lax.psum((tile_keys, tile_values), 'resp')  153 us
    reduce_scatter x1, waiting for transfers between devices, per_device(): lax.psum_scatter(buffers[1], 'ctx', scatter_dimension=0, tiled=True)  113 us
    reduce_scatter x1, waiting for transfers between devices, per_device(): lax.psum_scatter(buffers[2], 'resp', scatter_dimension=0, tiled=True)  93.1 us
    reduce_scatter x1, waiting for transfers between devices, per_device(): lax.psum_scatter(buffers[3], 'resp', scatter_dimension=0, tiled=True)  90.1 us
    all_gather x1, blocking collectives, per_device(): lax.all_gather(prompt_keys, 'ctx', axis=0, tiled=True)  53.7 us
    all_gather x1, blocking collectives, per_device(): lax.all_gather(prompt_values, 'ctx', axis=0, tiled=True)  48.7 us
    all_gather x1, blocking collectives, per_device(): lax.all_gather(resp_keys, 'resp', axis=1, tiled=True)  46.4 us
  transfers between devices with their start and end apart: 5, of which 5 were waited for; matrix products, arithmetic and copies ran while one was open for 0% of the time, Pallas kernels for 0%

commit v1 on v0

v1 whole, which is shorter than its diff:
```python
import math

import jax
import jax.numpy as jnp
from jax import lax
from jax.experimental import pallas as pl
from jax.experimental.pallas import tpu as pltpu
from jax.sharding import PartitionSpec as P

HEAD = 128
HEADS = 8
BLOCK = 128
ROWS = BLOCK * HEADS
CHUNK = 512
PROMPT = 2048
LEN = 2048
WIDE = 2 * HEAD
SCALE = 1.0 / math.sqrt(HEAD)
EXP2_SCALE = SCALE * math.log2(math.e)
MIB = 1024 * 1024

AXES = ("y", "zh", "core", "zl", "x")
CTX = ("y", "zh", "core")
RESP = ("zl", "x")
NEAR = ("y", "core")

F32 = jnp.float32
BF16 = jnp.bfloat16


def load_rows(q_rows, q_ref):
    for h in range(HEADS):
        q_rows[h * BLOCK:(h + 1) * BLOCK, :] = q_ref[:, h * HEAD:(h + 1) * HEAD]


def fold(op, values):
    return op(values.reshape(values.shape[0] // 8, 8, ROWS), 0)


def scores_of(keys, q_rows):
    return lax.dot_general(keys, q_rows[...], (((1,), (1,)), ((), ())), preferred_element_type=F32)


def resp_rows(refs, j):
    rows = pl.ds(pl.multiple_of(j * BLOCK, BLOCK), BLOCK)
    return jnp.concatenate([ref[rows, at:at + HEAD] for ref, at in refs], 0)


def key_refs(r0, r1, r2k, r3):
    return ((r0, 0), (r1, 0), (r2k, 0), (r3, 0))


def value_refs(r0, r1, r2v, r3):
    return ((r0, HEAD), (r1, HEAD), (r2v, 0), (r3, HEAD))


def masked_scores(keys, q_rows, zl, x):
    s = scores_of(keys, q_rows)
    row = lax.broadcasted_iota(jnp.int32, (CHUNK, ROWS), 0)
    key_pos = ((x - row // BLOCK) & 3) * BLOCK + row % BLOCK
    query_pos = x * BLOCK + lax.broadcasted_iota(jnp.int32, (CHUNK, ROWS), 1) % BLOCK
    return jnp.where(key_pos <= query_pos, s, -1e30)


def resp_forward_kernel(place, q_ref, r0, r1, r2k, r2v, r3, top_ref, total_ref, acc_ref, q_rows, s_all):
    keys = key_refs(r0, r1, r2k, r3)
    values = value_refs(r0, r1, r2v, r3)
    zl, x = place[0], place[1]
    load_rows(q_rows, q_ref)

    s = masked_scores(resp_rows(keys, 0), q_rows, zl, x)
    s_all[0:CHUNK, :] = s
    top_ref[...] = fold(jnp.max, s)

    def score_step(j, carry):
        s = scores_of(resp_rows(keys, j), q_rows)
        s_all[pl.ds(pl.multiple_of(j * CHUNK, CHUNK), CHUNK), :] = s
        top_ref[...] = jnp.maximum(top_ref[...], fold(jnp.max, s))
        return carry

    lax.fori_loop(1, zl + 1, score_step, 0)
    peak = jnp.max(top_ref[...], 0, keepdims=True)
    total_ref[...] = jnp.zeros(total_ref.shape, F32)
    acc_ref[...] = jnp.zeros(acc_ref.shape, F32)

    def weight_step(j, carry):
        at = pl.ds(pl.multiple_of(j * CHUNK, CHUNK), CHUNK)
        e = jnp.exp2((s_all[at, :] - peak) * EXP2_SCALE)
        total_ref[...] += fold(jnp.sum, e)
        acc_ref[...] += jnp.dot(resp_rows(values, j).T, e.astype(BF16), preferred_element_type=F32)
        return carry

    lax.fori_loop(0, zl + 1, weight_step, 0)


def prompt_kernel(place, q_ref, c_ref, pkv_ref, rtop_ref, rtotal_ref, racc_ref,
                  out_ref, pg_ref, dq_ref, c_cols, delta_ref, peak_ref,
                  q_rows, c_rows, s_all, e_all, top, total, acc):
    first = (place[0] * 4 + place[1]) * BLOCK
    length = place[2]
    steps = PROMPT // CHUNK
    load_rows(q_rows, q_ref)
    top[...] = rtop_ref[...]

    def rows_of(i):
        return pl.ds(pl.multiple_of(i * CHUNK, CHUNK), CHUNK)

    def score_step(i, carry):
        s = scores_of(pkv_ref[rows_of(i), 0:HEAD], q_rows)
        s_all[rows_of(i), :] = s
        top[...] = jnp.maximum(top[...], fold(jnp.max, s))
        return carry

    lax.fori_loop(0, steps, score_step, 0)
    peak = jnp.max(top[...], 0, keepdims=True)
    peak_ref[...] = peak
    share = jnp.exp2((jnp.max(rtop_ref[...], 0, keepdims=True) - peak) * EXP2_SCALE)
    total[...] = rtotal_ref[...] * share
    acc[...] = racc_ref[...] * share

    def weight_step(i, carry):
        e = jnp.exp2((s_all[rows_of(i), :] - peak) * EXP2_SCALE)
        total[...] += fold(jnp.sum, e)
        e = e.astype(BF16)
        e_all[rows_of(i), :] = e
        acc[...] += jnp.dot(pkv_ref[rows_of(i), HEAD:WIDE].T, e, preferred_element_type=F32)
        return carry

    lax.fori_loop(0, steps, weight_step, 0)
    inverse = 1.0 / jnp.sum(total[...], 0, keepdims=True)

    for h in range(HEADS):
        cols = slice(h * BLOCK, (h + 1) * BLOCK)
        query_pos = first + lax.broadcasted_iota(jnp.int32, (HEAD, BLOCK), 1)
        valid = query_pos < length
        inv = inverse[:, cols]
        out = jnp.where(valid, acc[:, cols] * inv, 0.0)
        out_ref[:, h * HEAD:(h + 1) * HEAD] = out.T.astype(BF16)
        cot = c_ref[:, h * HEAD:(h + 1) * HEAD].astype(F32).T
        cot = jnp.where(valid, cot * inv, 0.0)
        cot16 = cot.astype(BF16)
        c_cols[:, cols] = cot16
        c_rows[cols, :] = cot16.astype(F32).T.astype(BF16)
        delta_ref[:, cols] = jnp.sum(cot16.astype(F32) * out, 0, keepdims=True)
    delta = delta_ref[...]
    dq_ref[...] = jnp.zeros(dq_ref.shape, F32)

    def grad_step(i, carry):
        keys = pkv_ref[rows_of(i), 0:HEAD]
        values = pkv_ref[rows_of(i), HEAD:WIDE]
        e = e_all[rows_of(i), :]
        dp = jnp.dot(values, c_cols[...], preferred_element_type=F32)
        ds = (dp - delta).astype(BF16) * e
        dq_ref[...] += jnp.dot(keys.T, ds, preferred_element_type=F32)
        dk = jnp.dot(ds, q_rows[...], preferred_element_type=F32) * SCALE
        dv = jnp.dot(e, c_rows[...], preferred_element_type=F32)
        pg_ref[rows_of(i), 0:HEAD] = dk.astype(BF16)
        pg_ref[rows_of(i), HEAD:WIDE] = dv.astype(BF16)
        return carry

    lax.fori_loop(0, steps, grad_step, 0)


def resp_backward_kernel(place, q_ref, r0, r1, r2k, r2v, r3, c_cols, delta_ref, peak_ref, dqp_ref,
                         dq_ref, rg_ref, q_rows, c_rows, acc):
    key_at = key_refs(r0, r1, r2k, r3)
    value_at = value_refs(r0, r1, r2v, r3)
    zl, x = place[0], place[1]
    load_rows(q_rows, q_ref)
    for h in range(HEADS):
        cols = slice(h * BLOCK, (h + 1) * BLOCK)
        c_rows[cols, :] = c_cols[:, cols].astype(F32).T.astype(BF16)
    acc[...] = dqp_ref[...]
    delta = delta_ref[...]
    peak = peak_ref[...]

    def grad_step(j, keys, s):
        e = jnp.exp2((s - peak) * EXP2_SCALE).astype(BF16)
        dp = jnp.dot(resp_rows(value_at, j), c_cols[...], preferred_element_type=F32)
        ds = (dp - delta).astype(BF16) * e
        acc[...] += jnp.dot(keys.T, ds, preferred_element_type=F32)
        dk = (jnp.dot(ds, q_rows[...], preferred_element_type=F32) * SCALE).astype(BF16)
        dv = jnp.dot(e, c_rows[...], preferred_element_type=F32).astype(BF16)
        at = pl.ds(pl.multiple_of(j * BLOCK, BLOCK), BLOCK)
        for i in range(4):
            rows = slice(i * BLOCK, (i + 1) * BLOCK)
            rg_ref[(4 - i) % 4, at, 0:HEAD] = dk[rows]
            rg_ref[(4 - i) % 4, at, HEAD:WIDE] = dv[rows]

    keys = resp_rows(key_at, 0)
    grad_step(0, keys, masked_scores(keys, q_rows, zl, x))

    def full_step(j, carry):
        keys = resp_rows(key_at, j)
        grad_step(j, keys, scores_of(keys, q_rows))
        return carry

    lax.fori_loop(1, zl + 1, full_step, 0)
    for h in range(HEADS):
        dq = acc[:, h * BLOCK:(h + 1) * BLOCK] * SCALE
        dq_ref[:, h * HEAD:(h + 1) * HEAD] = dq.T.astype(BF16)


def call(kernel, args, outs, scratch, matmuls, keys):
    smem = pl.BlockSpec(memory_space=pltpu.SMEM)
    vmem = pl.BlockSpec(memory_space=pltpu.VMEM)
    return pl.pallas_call(
        kernel,
        out_shape=tuple(jax.ShapeDtypeStruct(shape, dtype) for shape, dtype in outs),
        in_specs=[smem] + [vmem] * (len(args) - 1),
        out_specs=(vmem,) * len(outs),
        scratch_shapes=[pltpu.VMEM(shape, dtype) for shape, dtype in scratch],
        compiler_params=pltpu.CompilerParams(vmem_limit_bytes=32 * MIB),
        cost_estimate=pl.CostEstimate(
            flops=2 * matmuls * ROWS * keys * HEAD,
            bytes_accessed=6 * MIB,
            transcendentals=ROWS * keys,
        ),
    )(*args)


def exchange(blocks, axes):
    return lax.all_to_all(blocks, axes, 0, 0, tiled=True)


def gather(own, axes, count):
    return exchange(jnp.broadcast_to(own[None], (count,) + own.shape), axes)


def around_x(block, shift):
    return lax.ppermute(block, "x", [(x, (x + shift) % 4) for x in range(4)])


def along_zl(block, shift):
    return lax.ppermute(block, "zl", [(z, z + shift) for z in range(4) if 0 <= z + shift < 4])


def swap_zl(block, bit):
    return lax.ppermute(block, "zl", [(z, z ^ bit) for z in range(4)])


def total_of(parts):
    terms = [parts[i].astype(F32) for i in range(len(parts))]
    while len(terms) > 1:
        terms = [terms[i] + terms[i + 1] for i in range(0, len(terms), 2)]
    return terms[0]


def per_device(queries, resp_keys, resp_values, prompt_keys, prompt_values, cotangent, lengths):
    place = jnp.stack([lax.axis_index("zl"), lax.axis_index("x"), lengths[0]]).astype(jnp.int32)
    queries = queries[0]
    cotangent = cotangent[0]

    own_prompt = jnp.concatenate([prompt_keys, prompt_values], 1)
    own_resp = jnp.concatenate([resp_keys[0], resp_values[0]], 1)
    far = gather(own_prompt, "zh", 4).reshape(PROMPT // 8, WIDE)
    below = [along_zl(own_resp, k) for k in (1, 2, 3)]
    far, *below = lax.optimization_barrier((far, *below))

    pkv = gather(far, NEAR, 8).reshape(PROMPT, WIDE)
    r0 = jnp.concatenate([own_resp] + below, 0)
    r1 = around_x(r0, 1)
    r3 = around_x(r0, 3)
    r2k = around_x(r1[:, :HEAD], 1)
    r2v = around_x(r3[:, HEAD:], 3)
    rkv = [r0, r1, r2k, r2v, r3]

    rtop, rtotal, racc = call(
        resp_forward_kernel,
        [place, queries] + rkv,
        [((8, ROWS), F32), ((8, ROWS), F32), ((HEAD, ROWS), F32)],
        [((ROWS, HEAD), BF16), ((LEN, ROWS), F32)],
        2,
        LEN,
    )
    out, pgrad, dq_prompt, cols, delta, peak = call(
        prompt_kernel,
        [place, queries, cotangent, pkv, rtop, rtotal, racc],
        [((BLOCK, ROWS), BF16), ((PROMPT, WIDE), BF16), ((HEAD, ROWS), F32), ((HEAD, ROWS), BF16),
         ((1, ROWS), F32), ((1, ROWS), F32)],
        [((ROWS, HEAD), BF16), ((ROWS, HEAD), BF16), ((PROMPT, ROWS), F32), ((PROMPT, ROWS), BF16),
         ((8, ROWS), F32), ((8, ROWS), F32), ((HEAD, ROWS), F32)],
        6,
        PROMPT,
    )
    dq, rgrad = call(
        resp_backward_kernel,
        [place, queries] + rkv + [cols, delta, peak, dq_prompt],
        [((BLOCK, ROWS), BF16), ((4, LEN // 4, WIDE), BF16)],
        [((ROWS, HEAD), BF16), ((ROWS, HEAD), BF16), ((HEAD, ROWS), F32)],
        5,
        LEN,
    )

    near, _ = lax.optimization_barrier((exchange(pgrad.reshape(8, PROMPT // 8, WIDE), NEAR), rgrad))
    part = total_of(near).astype(BF16)
    part = total_of(exchange(part.reshape(4, PROMPT // 32, WIDE), "zh")).astype(BF16)

    column = total_of([rgrad[0]] + [around_x(rgrad[k], k) for k in (1, 2, 3)])
    sent = column.astype(BF16)
    down = [along_zl(sent[k * BLOCK:(k + 1) * BLOCK], -k) for k in (1, 2, 3)]
    grad_resp = total_of([column[:BLOCK]] + down)

    ring = [part] + [around_x(part, k) for k in (1, 2, 3)]
    part = total_of([ring[0], ring[2], ring[1], ring[3]]).astype(BF16)
    part = total_of([part, swap_zl(part, 1)]).astype(BF16)
    grad_prompt = total_of([part, swap_zl(part, 2)])
    return (
        out[None],
        dq[None],
        grad_resp[None, :, :HEAD],
        grad_resp[None, :, HEAD:],
        grad_prompt[:, :HEAD],
        grad_prompt[:, HEAD:],
    )


def solution(mesh):
    fine = jax.sharding.Mesh(mesh.devices.reshape(4, 4, 2, 4, 4), AXES)
    rows = P(CTX, RESP, None)
    return jax.shard_map(
        per_device,
        mesh=fine,
        in_specs=(rows, rows, rows, P(CTX, None), P(CTX, None), rows, P(CTX)),
        out_specs=(rows, rows, rows, rows, P(CTX, None), P(CTX, None)),
        check_vma=False,
    )
```

time: 1100 us -> 151 us (0.14)
  the two profiles are of different devices: /device:TPU:16 before, /device:TPU:40 now
where the time goes in v1:
time: 151 us; the launch traced here: 150 us
  starting transfers between devices  84.4 us (56%)
  waiting for transfers between devices  39.3 us (26%)
  Pallas kernels  17.9 us (12%)
  local copies, waits for them, and re-layouts  3.92 us (3%)
  other arithmetic  3.16 us (2%)
  between operations  1.59 us (1%)
    ppermute x10, starting transfers between devices, around_x(): return lax.ppermute(block, 'x', [(x, (x + shift) % 4) for x in range(4)])  34 us
    all_to_all x4, starting transfers between devices, exchange(): return lax.all_to_all(blocks, axes, 0, 0, tiled=True)  32.5 us
    pallas_call x3, Pallas kernels, call(): pl.pallas_call(kernel, out_shape=tuple((jax.ShapeDtypeStruct(shape, dtype...  17.9 us
    all_to_all x4, waiting for transfers between devices, exchange(): return lax.all_to_all(blocks, axes, 0, 0, tiled=True)  16 us
    ppermute x6, waiting for transfers between devices, along_zl(): lax.ppermute(block, 'zl', [(z, z + shift) for z in range(4) if 0 <= z + s...  12.8 us
    ppermute x6, starting transfers between devices, along_zl(): lax.ppermute(block, 'zl', [(z, z + shift) for z in range(4) if 0 <= z + s...  10.5 us
    ppermute x10, waiting for transfers between devices, around_x(): return lax.ppermute(block, 'x', [(x, (x + shift) % 4) for x in range(4)])  9.36 us
    ppermute x2, starting transfers between devices, swap_zl(): return lax.ppermute(block, 'zl', [(z, z ^ bit) for z in range(4)])  7.43 us
  transfers between devices with their start and end apart: 22, of which 10 were waited for; matrix products, arithmetic and copies ran while one was open for 2% of the time, Pallas kernels for 5%

profile of v1, /device:TPU:40, one launch (start us, length us, event | category | flops | bytes accessed | tf_op | source)
XLA Modules:
  0.0 150.3 jit_solution(14997327921202603714)
XLA Ops:
  2.0 14.3 %all-to-all-start = ((bf16[4,64,256]{2,1,0:T(8,128)(2,1)}), bf16[4,64,256]{2,1,0:T(8,128)(2,1)S(1)}, u32[]{:S(2)}, u32[]{:S(2)}) async-start(bf16[4,64,256]{2,1,0:T(8,128)(2,1)} %broadcast_in_dim.24), calls=%async_computation | async-start | bytes 262144 | tf_op jit(solution)/shard_map/all_to_all | solution.py:223
  17.1 4.0 %collective-permute-start.1 = (bf16[128,256]{1,0:T(8,128)(2,1)S(1)}, bf16[128,256]{1,0:T(8,128)(2,1)S(1)}, u32[]{:S(2)}, u32[]{:S(2)}) collective-permute-start(bf16[128,256]{1,0:T(8,128)(2,1)S(1)} %pad_maximum_fusion.1), channel_id=1, source_target_pairs={{0,8},{4,12},{1,9},{5,13},{2,10},{6,14},{3,11},{7,15},{16,24},{20,... | collective-permute-start | bytes 196616 | tf_op jit(solution)/shard_map/ppermute | solution.py:235
  23.0 4.8 %collective-permute-done.1 = bf16[128,256]{1,0:T(8,128)(2,1)S(1)} collective-permute-done((bf16[128,256]{1,0:T(8,128)(2,1)S(1)}, bf16[128,256]{1,0:T(8,128)(2,1)S(1)}, u32[]{:S(2)}, u32[]{:S(2)}) %collective-permute-start.1) | collective-permute-done | bytes 65568 | tf_op jit(solution)/shard_map/ppermute | solution.py:235
  31.9 4.9 %all-to-all-start.1 = ((bf16[8,256,256]{2,1,0:T(8,128)(2,1)}), bf16[8,256,256]{2,1,0:T(8,128)(2,1)S(1)}, u32[]{:S(2)}, u32[]{:S(2)}) async-start(bf16[8,256,256]{2,1,0:T(8,128)(2,1)} %broadcast_in_dim.25), calls=%async_computation.1 | async-start | bytes 2097152 | tf_op jit(solution)/shard_map/all_to_all | solution.py:223
  36.9 4.8 %collective-permute-start.5 = (bf16[512,256]{1,0:T(8,128)(2,1)S(1)}, bf16[512,256]{1,0:T(8,128)(2,1)S(1)}, u32[]{:S(2)}, u32[]{:S(2)}) collective-permute-start(bf16[512,256]{1,0:T(8,128)(2,1)S(1)} %pad_maximum_fusion.r0), channel_id=1, source_target_pairs={{0,3},{1,0},{2,1},{3,2},{4,7},{5,4},{6,5},{7,6},{8,11},{9,8},{10,9... | collective-permute-start | bytes 786440 | tf_op jit(solution)/shard_map/ppermute | solution.py:231
  43.6 3.9 %collective-permute-done.5.r3 = bf16[512,256]{1,0:T(8,128)(2,1)S(1)} collective-permute-done((bf16[512,256]{1,0:T(8,128)(2,1)S(1)}, bf16[512,256]{1,0:T(8,128)(2,1)S(1)}, u32[]{:S(2)}, u32[]{:S(2)}) %collective-permute-start.5) | collective-permute-done | bytes 262176 | tf_op jit(solution)/shard_map/ppermute | solution.py:231
  47.5 5.6 %collective-permute-start.6 = (bf16[512,128]{1,0:T(8,128)(2,1)S(1)}, bf16[512,128]{1,0:T(8,128)(2,1)S(1)}, u32[]{:S(2)}, u32[]{:S(2)}) collective-permute-start(bf16[512,128]{1,0:T(8,128)(2,1)S(1)} %slice.105), channel_id=1, source_target_pairs={{0,3},{1,0},{2,1},{3,2},{4,7},{5,4},{6,5},{7,6},{8,11},{9,8},{10,9... | collective-permute-start | bytes 393224 | tf_op jit(solution)/shard_map/ppermute | solution.py:231
  53.2 1.9 %collective-permute-start.4 = (bf16[512,128]{1,0:T(8,128)(2,1)S(1)}, bf16[512,128]{1,0:T(8,128)(2,1)S(1)}, u32[]{:S(2)}, u32[]{:S(2)}) collective-permute-start(bf16[512,128]{1,0:T(8,128)(2,1)S(1)} %slice.104), channel_id=1, source_target_pairs={{0,1},{1,2},{2,3},{3,0},{4,5},{5,6},{6,7},{7,4},{8,9},{9,10},{10,1... | collective-permute-start | bytes 393224 | tf_op jit(solution)/shard_map/ppermute | solution.py:231
  55.8 5.4 %collective-permute-done.4.r2k = bf16[512,128]{1,0:T(8,128)(2,1)S(1)} collective-permute-done((bf16[512,128]{1,0:T(8,128)(2,1)S(1)}, bf16[512,128]{1,0:T(8,128)(2,1)S(1)}, u32[]{:S(2)}, u32[]{:S(2)}) %collective-permute-start.4) | collective-permute-done | bytes 131104 | tf_op jit(solution)/shard_map/ppermute | solution.py:231
  61.3 2.6 %shard_map.118 = (f32[8,1024]{1,0:T(8,128)S(1)}, f32[8,1024]{1,0:T(8,128)S(1)}, f32[128,1024]{1,0:T(8,128)S(1)}) custom-call(s32[3]{0:T(128)S(1)} %pad_add_fusion.place, bf16[128,1024]{1,0:T(8,128)(2,1)S(1)} %bitcast.32, bf16[512,256]{1,0:T(8,128)(2,1)S(1)} %pad_maximum_fusion.r0, bf16[512,256]{1,0:T(8,128)(2,1)S(1)} %collective-permute-done.3.r1, ...), custom_call_target="tpu_custom_call" | custom-call | flops 1073741824 | bytes 6291456 | tf_op jit(solution)/shard_map/pallas_call | solution.py:207
  63.9 10.8 %shard_map.119 = (bf16[128,1024]{1,0:T(8,128)(2,1)}, bf16[2048,256]{1,0:T(8,128)(2,1)}, f32[128,1024]{1,0:T(8,128)S(1)}, bf16[128,1024]{1,0:T(8,128)(2,1)S(1)}, ...) custom-call(s32[3]{0:T(128)S(1)} %pad_add_fusion.place, bf16[128,1024]{1,0:T(8,128)(2,1)S(1)} %bitcast.33, ...), custom_call_target="tpu_custom_call" | custom-call | flops 3221225472 | bytes 6291456 | tf_op jit(solution)/shard_map/pallas_call | solution.py:207
  75.4 4.9 %all-to-all-start.2 = ((bf16[8,256,256]{2,1,0:T(8,128)(2,1)}), bf16[8,256,256]{2,1,0:T(8,128)(2,1)}, u32[]{:S(2)}, u32[]{:S(2)}) async-start(bf16[8,256,256]{2,1,0:T(8,128)(2,1)} %bitcast.16), calls=%async_computation.2 | async-start | bytes 2097152 | tf_op jit(solution)/shard_map/all_to_all | solution.py:223
  80.4 4.5 %shard_map.120 = (bf16[128,1024]{1,0:T(8,128)(2,1)}, bf16[4,512,256]{2,1,0:T(8,128)(2,1)S(1)}) custom-call(s32[3]{0:T(128)S(1)} %pad_add_fusion.place, bf16[128,1024]{1,0:T(8,128)(2,1)S(1)} %bitcast.34, bf16[512,256]{1,0:T(8,128)(2,1)S(1)} %pad_maximum_fusion.r0, bf16[512,256]{1,0:T(8,128)(2,1)S(1)} %collective-permute-done.3.r1, ...), custom_call_target="tpu_custom_call" | custom-call | flops 2684354560 | bytes 6291456 | tf_op jit(solution)/shard_map/pallas_call | solution.py:207
  85.0 1.9 %collective-permute-start.7 = (bf16[512,256]{1,0:T(8,128)(2,1)S(1)}, bf16[512,256]{1,0:T(8,128)(2,1)S(1)}, u32[]{:S(2)}, u32[]{:S(2)}) collective-permute-start(bf16[512,256]{1,0:T(8,128)(2,1)S(1)} %get-tuple-element.40), channel_id=1, source_target_pairs={{0,1},{1,2},{2,3},{3,0},{4,5},{5,6},{6,7},{7,4},{8,9},{9,10},{10,1... | collective-permute-start | bytes 786440 | tf_op jit(solution)/shard_map/ppermute | solution.py:231
  86.9 5.1 %collective-permute-start.9 = (bf16[512,256]{1,0:T(8,128)(2,1)S(1)}, bf16[512,256]{1,0:T(8,128)(2,1)S(1)}, u32[]{:S(2)}, u32[]{:S(2)}) collective-permute-start(bf16[512,256]{1,0:T(8,128)(2,1)S(1)} %get-tuple-element.41), channel_id=1, source_target_pairs={{0,3},{1,0},{2,1},{3,2},{4,7},{5,4},{6,5},{7,6},{8,11},{9,8},{10,9... | collective-permute-start | bytes 786440 | tf_op jit(solution)/shard_map/ppermute | solution.py:231
  95.0 2.1 %add_convert_fusion = bf16[1,256,256]{2,1,0:T(8,128)(2,1)} fusion(bf16[8,256,256]{2,1,0:T(8,128)(2,1)} %all-to-all-done.2), kind=kLoop, calls=%fused_computation.3 | loop fusion | flops 1048576 | bytes 1179648 | tf_op jit(solution)/shard_map/convert.1
  97.1 8.4 %all-to-all-start.3 = ((bf16[4,64,256]{2,1,0:T(8,128)(2,1)}), bf16[4,64,256]{2,1,0:T(8,128)(2,1)S(1)}, u32[]{:S(2)}, u32[]{:S(2)}) async-start(bf16[4,64,256]{2,1,0:T(8,128)(2,1)} %bitcast.17), calls=%async_computation.3 | async-start | bytes 262144 | tf_op jit(solution)/shard_map/all_to_all | solution.py:223
  105.6 13.5 %all-to-all-done.3 = bf16[4,64,256]{2,1,0:T(8,128)(2,1)S(1)} async-done(((bf16[4,64,256]{2,1,0:T(8,128)(2,1)}), bf16[4,64,256]{2,1,0:T(8,128)(2,1)S(1)}, u32[]{:S(2)}, u32[]{:S(2)}) %all-to-all-start.3) | async-done | bytes 131104 | tf_op jit(solution)/shard_map/all_to_all | solution.py:223
  121.0 4.3 %collective-permute-start.13 = (bf16[64,256]{1,0:T(8,128)(2,1)S(1)}, bf16[64,256]{1,0:T(8,128)(2,1)S(1)}, u32[]{:S(2)}, u32[]{:S(2)}) collective-permute-start(bf16[64,256]{1,0:T(8,128)(2,1)S(1)} %fusion.2), channel_id=1, source_target_pairs={{0,2},{1,3},{2,0},{3,1},{4,6},{5,7},{6,4},{7,5},{8,10},{9,11},{10,... | collective-permute-start | bytes 98312 | tf_op jit(solution)/shard_map/ppermute | solution.py:231
  125.4 4.5 %collective-permute-start.15 = (bf16[64,256]{1,0:T(8,128)(2,1)S(1)}, bf16[64,256]{1,0:T(8,128)(2,1)S(1)}, u32[]{:S(2)}, u32[]{:S(2)}) collective-permute-start(bf16[64,256]{1,0:T(8,128)(2,1)S(1)} %fusion.2), channel_id=1, source_target_pairs={{0,3},{1,0},{2,1},{3,2},{4,7},{5,4},{6,5},{7,6},{8,11},{9,8},{10,9... | collective-permute-start | bytes 98312 | tf_op jit(solution)/shard_map/ppermute | solution.py:231
  129.9 1.9 %collective-permute-start.10 = (bf16[128,256]{1,0:T(8,128)(2,1)S(1)}, bf16[128,256]{1,0:T(8,128)(2,1)S(1)}, u32[]{:S(2)}, u32[]{:S(2)}) collective-permute-start(bf16[128,256]{1,0:T(8,128)(2,1)S(1)} %get-tuple-element.43), channel_id=1, source_target_pairs={{4,0},{8,4},{12,8},{5,1},{9,5},{13,9},{6,2},{10,6},{14,10},{7,3},{... | collective-permute-start | bytes 196616 | tf_op jit(solution)/shard_map/ppermute | solution.py:235
  135.8 2.3 %collective-permute-done.10 = bf16[128,256]{1,0:T(8,128)(2,1)S(1)} collective-permute-done((bf16[128,256]{1,0:T(8,128)(2,1)S(1)}, bf16[128,256]{1,0:T(8,128)(2,1)S(1)}, u32[]{:S(2)}, u32[]{:S(2)}) %collective-permute-start.10) | collective-permute-done | bytes 65568 | tf_op jit(solution)/shard_map/ppermute | solution.py:235
  138.1 4.1 %collective-permute-done.11 = bf16[128,256]{1,0:T(8,128)(2,1)S(1)} collective-permute-done((bf16[128,256]{1,0:T(8,128)(2,1)S(1)}, bf16[128,256]{1,0:T(8,128)(2,1)S(1)}, u32[]{:S(2)}, u32[]{:S(2)}) %collective-permute-start.11) | collective-permute-done | bytes 65568 | tf_op jit(solution)/shard_map/ppermute | solution.py:235
  142.3 5.5 %collective-permute-start.17 = (bf16[64,256]{1,0:T(8,128)(2,1)S(1)}, bf16[64,256]{1,0:T(8,128)(2,1)S(1)}, u32[]{:S(2)}, u32[]{:S(2)}) collective-permute-start(bf16[64,256]{1,0:T(8,128)(2,1)S(1)} %add_convert_fusion.1), channel_id=1, source_target_pairs={{0,8},{4,12},{8,0},{12,4},{1,9},{5,13},{9,1},{13,5},{2,10},{6,14},... | collective-permute-start | bytes 98312 | tf_op jit(solution)/shard_map/ppermute | solution.py:239
  (54 shorter events, 22.6 us)
Async XLA Ops:
  2.0 14.3 %copy-start.5 = (bf16[1,128,128]{2,1,0:T(8,128)(2,1)S(1)}, bf16[1,128,128]{2,1,0:T(8,128)(2,1)}, u32[]{:S(2)}) copy-start(bf16[1,128,128]{2,1,0:T(8,128)(2,1)} %param.8) | copy-start | bytes 98308
  2.0 28.8 %all-to-all-start = ((bf16[4,64,256]{2,1,0:T(8,128)(2,1)}), bf16[4,64,256]{2,1,0:T(8,128)(2,1)S(1)}, u32[]{:S(2)}, u32[]{:S(2)}) async-start(bf16[4,64,256]{2,1,0:T(8,128)(2,1)} %broadcast_in_dim.24), calls=%async_computation | async-start | bytes 262144 | tf_op jit(solution)/shard_map/all_to_all | solution.py:223
  16.4 6.6 %collective-permute-start.2 = (bf16[128,256]{1,0:T(8,128)(2,1)S(1)}, bf16[128,256]{1,0:T(8,128)(2,1)S(1)}, u32[]{:S(2)}, u32[]{:S(2)}) collective-permute-start(bf16[128,256]{1,0:T(8,128)(2,1)S(1)} %pad_maximum_fusion.1), channel_id=1, source_target_pairs={{0,12},{1,13},{2,14},{3,15},{16,28},{17,29},{18,30},{19,31},{32,44... | collective-permute-start | bytes 196616 | tf_op jit(solution)/shard_map/ppermute | solution.py:235
  17.1 10.7 %collective-permute-start.1 = (bf16[128,256]{1,0:T(8,128)(2,1)S(1)}, bf16[128,256]{1,0:T(8,128)(2,1)S(1)}, u32[]{:S(2)}, u32[]{:S(2)}) collective-permute-start(bf16[128,256]{1,0:T(8,128)(2,1)S(1)} %pad_maximum_fusion.1), channel_id=1, source_target_pairs={{0,8},{4,12},{1,9},{5,13},{2,10},{6,14},{3,11},{7,15},{16,24},{20,... | collective-permute-start | bytes 196616 | tf_op jit(solution)/shard_map/ppermute | solution.py:235
  21.1 8.3 %collective-permute-start = (bf16[128,256]{1,0:T(8,128)(2,1)S(1)}, bf16[128,256]{1,0:T(8,128)(2,1)S(1)}, u32[]{:S(2)}, u32[]{:S(2)}) collective-permute-start(bf16[128,256]{1,0:T(8,128)(2,1)S(1)} %pad_maximum_fusion.1), channel_id=1, source_target_pairs={{0,4},{4,8},{8,12},{1,5},{5,9},{9,13},{2,6},{6,10},{10,14},{3,7},{... | collective-permute-start | bytes 196616 | tf_op jit(solution)/shard_map/ppermute | solution.py:235
  31.9 31.9 %all-to-all-start.1 = ((bf16[8,256,256]{2,1,0:T(8,128)(2,1)}), bf16[8,256,256]{2,1,0:T(8,128)(2,1)S(1)}, u32[]{:S(2)}, u32[]{:S(2)}) async-start(bf16[8,256,256]{2,1,0:T(8,128)(2,1)} %broadcast_in_dim.25), calls=%async_computation.1 | async-start | bytes 2097152 | tf_op jit(solution)/shard_map/all_to_all | solution.py:223
  36.9 24.4 %copy-start.1 = (bf16[1,128,1024]{2,1,0:T(8,128)(2,1)S(1)}, bf16[1,128,1024]{2,1,0:T(8,128)(2,1)}, u32[]{:S(2)}) copy-start(bf16[1,128,1024]{2,1,0:T(8,128)(2,1)} %param.7) | copy-start | bytes 786436
  36.9 10.7 %collective-permute-start.5 = (bf16[512,256]{1,0:T(8,128)(2,1)S(1)}, bf16[512,256]{1,0:T(8,128)(2,1)S(1)}, u32[]{:S(2)}, u32[]{:S(2)}) collective-permute-start(bf16[512,256]{1,0:T(8,128)(2,1)S(1)} %pad_maximum_fusion.r0), channel_id=1, source_target_pairs={{0,3},{1,0},{2,1},{3,2},{4,7},{5,4},{6,5},{7,6},{8,11},{9,8},{10,9... | collective-permute-start | bytes 786440 | tf_op jit(solution)/shard_map/ppermute | solution.py:231
  41.7 11.5 %collective-permute-start.3 = (bf16[512,256]{1,0:T(8,128)(2,1)S(1)}, bf16[512,256]{1,0:T(8,128)(2,1)S(1)}, u32[]{:S(2)}, u32[]{:S(2)}) collective-permute-start(bf16[512,256]{1,0:T(8,128)(2,1)S(1)} %pad_maximum_fusion.r0), channel_id=1, source_target_pairs={{0,1},{1,2},{2,3},{3,0},{4,5},{5,6},{6,7},{7,4},{8,9},{9,10},{10,1... | collective-permute-start | bytes 786440 | tf_op jit(solution)/shard_map/ppermute | solution.py:231
  47.5 8.3 %collective-permute-start.6 = (bf16[512,128]{1,0:T(8,128)(2,1)S(1)}, bf16[512,128]{1,0:T(8,128)(2,1)S(1)}, u32[]{:S(2)}, u32[]{:S(2)}) collective-permute-start(bf16[512,128]{1,0:T(8,128)(2,1)S(1)} %slice.105), channel_id=1, source_target_pairs={{0,3},{1,0},{2,1},{3,2},{4,7},{5,4},{6,5},{7,6},{8,11},{9,8},{10,9... | collective-permute-start | bytes 393224 | tf_op jit(solution)/shard_map/ppermute | solution.py:231
  53.2 8.1 %collective-permute-start.4 = (bf16[512,128]{1,0:T(8,128)(2,1)S(1)}, bf16[512,128]{1,0:T(8,128)(2,1)S(1)}, u32[]{:S(2)}, u32[]{:S(2)}) collective-permute-start(bf16[512,128]{1,0:T(8,128)(2,1)S(1)} %slice.104), channel_id=1, source_target_pairs={{0,1},{1,2},{2,3},{3,0},{4,5},{5,6},{6,7},{7,4},{8,9},{9,10},{10,1... | collective-permute-start | bytes 393224 | tf_op jit(solution)/shard_map/ppermute | solution.py:231
  75.4 19.6 %all-to-all-start.2 = ((bf16[8,256,256]{2,1,0:T(8,128)(2,1)}), bf16[8,256,256]{2,1,0:T(8,128)(2,1)}, u32[]{:S(2)}, u32[]{:S(2)}) async-start(bf16[8,256,256]{2,1,0:T(8,128)(2,1)} %bitcast.16), calls=%async_computation.2 | async-start | bytes 2097152 | tf_op jit(solution)/shard_map/all_to_all | solution.py:223
  85.0 20.4 %collective-permute-start.7 = (bf16[512,256]{1,0:T(8,128)(2,1)S(1)}, bf16[512,256]{1,0:T(8,128)(2,1)S(1)}, u32[]{:S(2)}, u32[]{:S(2)}) collective-permute-start(bf16[512,256]{1,0:T(8,128)(2,1)S(1)} %get-tuple-element.40), channel_id=1, source_target_pairs={{0,1},{1,2},{2,3},{3,0},{4,5},{5,6},{6,7},{7,4},{8,9},{9,10},{10,1... | collective-permute-start | bytes 786440 | tf_op jit(solution)/shard_map/ppermute | solution.py:231
  86.9 18.5 %collective-permute-start.9 = (bf16[512,256]{1,0:T(8,128)(2,1)S(1)}, bf16[512,256]{1,0:T(8,128)(2,1)S(1)}, u32[]{:S(2)}, u32[]{:S(2)}) collective-permute-start(bf16[512,256]{1,0:T(8,128)(2,1)S(1)} %get-tuple-element.41), channel_id=1, source_target_pairs={{0,3},{1,0},{2,1},{3,2},{4,7},{5,4},{6,5},{7,6},{8,11},{9,8},{10,9... | collective-permute-start | bytes 786440 | tf_op jit(solution)/shard_map/ppermute | solution.py:231
  92.1 13.4 %collective-permute-start.8 = (bf16[512,256]{1,0:T(8,128)(2,1)S(1)}, bf16[512,256]{1,0:T(8,128)(2,1)S(1)}, u32[]{:S(2)}, u32[]{:S(2)}) collective-permute-start(bf16[512,256]{1,0:T(8,128)(2,1)S(1)} %get-tuple-element.42), channel_id=1, source_target_pairs={{0,2},{1,3},{2,0},{3,1},{4,6},{5,7},{6,4},{7,5},{8,10},{9,11},{10,... | collective-permute-start | bytes 786440 | tf_op jit(solution)/shard_map/ppermute | solution.py:231
  97.1 22.0 %all-to-all-start.3 = ((bf16[4,64,256]{2,1,0:T(8,128)(2,1)}), bf16[4,64,256]{2,1,0:T(8,128)(2,1)S(1)}, u32[]{:S(2)}, u32[]{:S(2)}) async-start(bf16[4,64,256]{2,1,0:T(8,128)(2,1)} %bitcast.17), calls=%async_computation.3 | async-start | bytes 262144 | tf_op jit(solution)/shard_map/all_to_all | solution.py:223
  119.1 13.4 %collective-permute-start.14 = (bf16[64,256]{1,0:T(8,128)(2,1)S(1)}, bf16[64,256]{1,0:T(8,128)(2,1)S(1)}, u32[]{:S(2)}, u32[]{:S(2)}) collective-permute-start(bf16[64,256]{1,0:T(8,128)(2,1)S(1)} %fusion.2), channel_id=1, source_target_pairs={{0,1},{1,2},{2,3},{3,0},{4,5},{5,6},{6,7},{7,4},{8,9},{9,10},{10,1... | collective-permute-start | bytes 98312 | tf_op jit(solution)/shard_map/ppermute | solution.py:231
  121.0 12.8 %collective-permute-start.13 = (bf16[64,256]{1,0:T(8,128)(2,1)S(1)}, bf16[64,256]{1,0:T(8,128)(2,1)S(1)}, u32[]{:S(2)}, u32[]{:S(2)}) collective-permute-start(bf16[64,256]{1,0:T(8,128)(2,1)S(1)} %fusion.2), channel_id=1, source_target_pairs={{0,2},{1,3},{2,0},{3,1},{4,6},{5,7},{6,4},{7,5},{8,10},{9,11},{10,... | collective-permute-start | bytes 98312 | tf_op jit(solution)/shard_map/ppermute | solution.py:231
  125.4 8.5 %collective-permute-start.15 = (bf16[64,256]{1,0:T(8,128)(2,1)S(1)}, bf16[64,256]{1,0:T(8,128)(2,1)S(1)}, u32[]{:S(2)}, u32[]{:S(2)}) collective-permute-start(bf16[64,256]{1,0:T(8,128)(2,1)S(1)} %fusion.2), channel_id=1, source_target_pairs={{0,3},{1,0},{2,1},{3,2},{4,7},{5,4},{6,5},{7,6},{8,11},{9,8},{10,9... | collective-permute-start | bytes 98312 | tf_op jit(solution)/shard_map/ppermute | solution.py:231
  129.9 8.2 %collective-permute-start.10 = (bf16[128,256]{1,0:T(8,128)(2,1)S(1)}, bf16[128,256]{1,0:T(8,128)(2,1)S(1)}, u32[]{:S(2)}, u32[]{:S(2)}) collective-permute-start(bf16[128,256]{1,0:T(8,128)(2,1)S(1)} %get-tuple-element.43), channel_id=1, source_target_pairs={{4,0},{8,4},{12,8},{5,1},{9,5},{13,9},{6,2},{10,6},{14,10},{7,3},{... | collective-permute-start | bytes 196616 | tf_op jit(solution)/shard_map/ppermute | solution.py:235
  131.8 6.3 %collective-permute-start.12 = (bf16[128,256]{1,0:T(8,128)(2,1)S(1)}, bf16[128,256]{1,0:T(8,128)(2,1)S(1)}, u32[]{:S(2)}, u32[]{:S(2)}) collective-permute-start(bf16[128,256]{1,0:T(8,128)(2,1)S(1)} %get-tuple-element.44), channel_id=1, source_target_pairs={{12,0},{13,1},{14,2},{15,3},{28,16},{29,17},{30,18},{31,19},{44,32... | collective-permute-start | bytes 196616 | tf_op jit(solution)/shard_map/ppermute | solution.py:235
  132.5 9.7 %collective-permute-start.11 = (bf16[128,256]{1,0:T(8,128)(2,1)S(1)}, bf16[128,256]{1,0:T(8,128)(2,1)S(1)}, u32[]{:S(2)}, u32[]{:S(2)}) collective-permute-start(bf16[128,256]{1,0:T(8,128)(2,1)S(1)} %get-tuple-element.45), channel_id=1, source_target_pairs={{8,0},{12,4},{9,1},{13,5},{10,2},{14,6},{11,3},{15,7},{24,16},{28,... | collective-permute-start | bytes 196616 | tf_op jit(solution)/shard_map/ppermute | solution.py:235
  133.9 8.3 %collective-permute-start.16 = (bf16[64,256]{1,0:T(8,128)(2,1)S(1)}, bf16[64,256]{1,0:T(8,128)(2,1)S(1)}, u32[]{:S(2)}, u32[]{:S(2)}) collective-permute-start(bf16[64,256]{1,0:T(8,128)(2,1)S(1)} %add_convert_fusion.2), channel_id=1, source_target_pairs={{0,4},{4,0},{8,12},{12,8},{1,5},{5,1},{9,13},{13,9},{2,6},{6,2},{1... | collective-permute-start | bytes 98312 | tf_op jit(solution)/shard_map/ppermute | solution.py:239
  142.3 7.4 %collective-permute-start.17 = (bf16[64,256]{1,0:T(8,128)(2,1)S(1)}, bf16[64,256]{1,0:T(8,128)(2,1)S(1)}, u32[]{:S(2)}, u32[]{:S(2)}) collective-permute-start(bf16[64,256]{1,0:T(8,128)(2,1)S(1)} %add_convert_fusion.1), channel_id=1, source_target_pairs={{0,8},{4,12},{8,0},{12,4},{1,9},{5,13},{9,1},{13,5},{2,10},{6,14},... | collective-permute-start | bytes 98312 | tf_op jit(solution)/shard_map/ppermute | solution.py:239
  (4 other events, 22.7 us)

commit v2 on v1

v2 whole, which is shorter than its diff:
```python
import math

import jax
import jax.numpy as jnp
from jax import lax
from jax.experimental import pallas as pl
from jax.experimental.pallas import tpu as pltpu
from jax.sharding import PartitionSpec as P

HEAD = 128
HEADS = 8
BLOCK = 128
ROWS = BLOCK * HEADS
CHUNK = 512
PROMPT = 2048
LEN = 2048
WIDE = 2 * HEAD
SCALE = 1.0 / math.sqrt(HEAD)
EXP2_SCALE = SCALE * math.log2(math.e)
MIB = 1024 * 1024

AXES = ("y", "zh", "core", "zl", "x")
CTX = ("y", "zh", "core")
RESP = ("zl", "x")
NEAR = ("y", "core")

F32 = jnp.float32
BF16 = jnp.bfloat16


def load_rows(q_rows, q_ref):
    for h in range(HEADS):
        q_rows[h * BLOCK:(h + 1) * BLOCK, :] = q_ref[:, h * HEAD:(h + 1) * HEAD]


def fold(op, values):
    return op(values.reshape(values.shape[0] // 8, 8, ROWS), 0)


def scores_of(keys, q_rows):
    return lax.dot_general(keys, q_rows[...], (((1,), (1,)), ((), ())), preferred_element_type=F32)


def resp_rows(refs, j, at):
    rows = pl.ds(pl.multiple_of(j * BLOCK, BLOCK), BLOCK)
    return jnp.concatenate([ref[rows, at:at + HEAD] for ref in refs], 0)


def chunk_at(i):
    return pl.ds(pl.multiple_of(i * CHUNK, CHUNK), CHUNK)


def masked_scores(keys, q_rows, x):
    s = scores_of(keys, q_rows)
    row = lax.broadcasted_iota(jnp.int32, (CHUNK, ROWS), 0)
    key_pos = ((x - row // BLOCK) & 3) * BLOCK + row % BLOCK
    query_pos = x * BLOCK + lax.broadcasted_iota(jnp.int32, (CHUNK, ROWS), 1) % BLOCK
    return jnp.where(key_pos <= query_pos, s, -1e30)


def prompt_forward_kernel(q_ref, pkv_ref, e_ref, top_ref, total_ref, acc_ref, q_rows, s_all):
    load_rows(q_rows, q_ref)
    top_ref[...] = jnp.full(top_ref.shape, -1e30, F32)

    def score_step(i, carry):
        s = scores_of(pkv_ref[chunk_at(i), 0:HEAD], q_rows)
        s_all[chunk_at(i), :] = s
        top_ref[...] = jnp.maximum(top_ref[...], fold(jnp.max, s))
        return carry

    lax.fori_loop(0, PROMPT // CHUNK, score_step, 0)
    peak = jnp.max(top_ref[...], 0, keepdims=True)
    total_ref[...] = jnp.zeros(total_ref.shape, F32)
    acc_ref[...] = jnp.zeros(acc_ref.shape, F32)

    def weight_step(i, carry):
        e = jnp.exp2((s_all[chunk_at(i), :] - peak) * EXP2_SCALE)
        total_ref[...] += fold(jnp.sum, e)
        e = e.astype(BF16)
        e_ref[chunk_at(i), :] = e
        acc_ref[...] += jnp.dot(pkv_ref[chunk_at(i), HEAD:WIDE].T, e, preferred_element_type=F32)
        return carry

    lax.fori_loop(0, PROMPT // CHUNK, weight_step, 0)


def middle_kernel(place, q_ref, c_ref, pkv_ref, r0, r1, r2, r3, e_ref, ptop_ref, ptotal_ref, pacc_ref,
                  out_ref, pg_ref, dq_ref, cols_ref, delta_ref, peak_ref,
                  q_rows, c_rows, c_cols, pdelta, s_all, top, total, acc):
    refs = (r0, r1, r2, r3)
    zl, x, length = place[0], place[1], place[2]
    first = (zl * 4 + x) * BLOCK
    load_rows(q_rows, q_ref)

    s = masked_scores(resp_rows(refs, 0, 0), q_rows, x)
    s_all[0:CHUNK, :] = s
    top[...] = jnp.maximum(ptop_ref[...], fold(jnp.max, s))

    def score_step(j, carry):
        s = scores_of(resp_rows(refs, j, 0), q_rows)
        s_all[chunk_at(j), :] = s
        top[...] = jnp.maximum(top[...], fold(jnp.max, s))
        return carry

    lax.fori_loop(1, zl + 1, score_step, 0)
    peak = jnp.max(top[...], 0, keepdims=True)
    peak_ref[...] = peak
    share = jnp.exp2((jnp.max(ptop_ref[...], 0, keepdims=True) - peak) * EXP2_SCALE)
    total[...] = ptotal_ref[...] * share
    acc[...] = pacc_ref[...] * share

    def weight_step(j, carry):
        e = jnp.exp2((s_all[chunk_at(j), :] - peak) * EXP2_SCALE)
        total[...] += fold(jnp.sum, e)
        acc[...] += jnp.dot(resp_rows(refs, j, HEAD).T, e.astype(BF16), preferred_element_type=F32)
        return carry

    lax.fori_loop(0, zl + 1, weight_step, 0)
    inverse = 1.0 / jnp.sum(total[...], 0, keepdims=True)

    for h in range(HEADS):
        cols = slice(h * BLOCK, (h + 1) * BLOCK)
        query_pos = first + lax.broadcasted_iota(jnp.int32, (HEAD, BLOCK), 1)
        valid = query_pos < length
        inv = inverse[:, cols]
        out = jnp.where(valid, acc[:, cols] * inv, 0.0)
        out_ref[:, h * HEAD:(h + 1) * HEAD] = out.T.astype(BF16)
        cot = c_ref[:, h * HEAD:(h + 1) * HEAD].astype(F32).T
        cot = jnp.where(valid, cot * inv, 0.0)
        cot16 = cot.astype(BF16)
        cols_ref[:, cols] = cot16
        delta_ref[:, cols] = jnp.sum(cot16.astype(F32) * out, 0, keepdims=True)
        cot16 = (cot * share[:, cols]).astype(BF16)
        c_cols[:, cols] = cot16
        c_rows[cols, :] = cot16.astype(F32).T.astype(BF16)
        pdelta[:, cols] = jnp.sum(cot16.astype(F32) * out, 0, keepdims=True)
    delta = pdelta[...]
    dq_ref[...] = jnp.zeros(dq_ref.shape, F32)

    def grad_step(i, carry):
        keys = pkv_ref[chunk_at(i), 0:HEAD]
        values = pkv_ref[chunk_at(i), HEAD:WIDE]
        e = e_ref[chunk_at(i), :]
        dp = jnp.dot(values, c_cols[...], preferred_element_type=F32)
        ds = (dp - delta).astype(BF16) * e
        dq_ref[...] += jnp.dot(keys.T, ds, preferred_element_type=F32)
        dk = jnp.dot(ds, q_rows[...], preferred_element_type=F32) * SCALE
        dv = jnp.dot(e, c_rows[...], preferred_element_type=F32)
        pg_ref[chunk_at(i), 0:HEAD] = dk.astype(BF16)
        pg_ref[chunk_at(i), HEAD:WIDE] = dv.astype(BF16)
        return carry

    lax.fori_loop(0, PROMPT // CHUNK, grad_step, 0)


def resp_backward_kernel(place, q_ref, r0, r1, r2, r3, c_cols, delta_ref, peak_ref, dqp_ref,
                         dq_ref, rg_ref, q_rows, c_rows, acc):
    refs = (r0, r1, r2, r3)
    zl, x = place[0], place[1]
    load_rows(q_rows, q_ref)
    for h in range(HEADS):
        cols = slice(h * BLOCK, (h + 1) * BLOCK)
        c_rows[cols, :] = c_cols[:, cols].astype(F32).T.astype(BF16)
    acc[...] = dqp_ref[...]
    delta = delta_ref[...]
    peak = peak_ref[...]

    def grad_step(j, keys, s):
        e = jnp.exp2((s - peak) * EXP2_SCALE).astype(BF16)
        dp = jnp.dot(resp_rows(refs, j, HEAD), c_cols[...], preferred_element_type=F32)
        ds = (dp - delta).astype(BF16) * e
        acc[...] += jnp.dot(keys.T, ds, preferred_element_type=F32)
        dk = (jnp.dot(ds, q_rows[...], preferred_element_type=F32) * SCALE).astype(BF16)
        dv = jnp.dot(e, c_rows[...], preferred_element_type=F32).astype(BF16)
        at = pl.ds(pl.multiple_of(j * BLOCK, BLOCK), BLOCK)
        for i in range(4):
            rows = slice(i * BLOCK, (i + 1) * BLOCK)
            rg_ref[(4 - i) % 4, at, 0:HEAD] = dk[rows]
            rg_ref[(4 - i) % 4, at, HEAD:WIDE] = dv[rows]

    keys = resp_rows(refs, 0, 0)
    grad_step(0, keys, masked_scores(keys, q_rows, x))

    def full_step(j, carry):
        keys = resp_rows(refs, j, 0)
        grad_step(j, keys, scores_of(keys, q_rows))
        return carry

    lax.fori_loop(1, zl + 1, full_step, 0)
    for h in range(HEADS):
        dq = acc[:, h * BLOCK:(h + 1) * BLOCK] * SCALE
        dq_ref[:, h * HEAD:(h + 1) * HEAD] = dq.T.astype(BF16)


def call(kernel, place, args, outs, scratch, matmuls, keys):
    smem = pl.BlockSpec(memory_space=pltpu.SMEM)
    vmem = pl.BlockSpec(memory_space=pltpu.VMEM)
    return pl.pallas_call(
        kernel,
        out_shape=tuple(jax.ShapeDtypeStruct(shape, dtype) for shape, dtype in outs),
        in_specs=[smem] * len(place) + [vmem] * len(args),
        out_specs=(vmem,) * len(outs),
        scratch_shapes=[pltpu.VMEM(shape, dtype) for shape, dtype in scratch],
        compiler_params=pltpu.CompilerParams(vmem_limit_bytes=32 * MIB),
        cost_estimate=pl.CostEstimate(
            flops=2 * matmuls * ROWS * keys * HEAD,
            bytes_accessed=6 * MIB,
            transcendentals=ROWS * keys,
        ),
    )(*place, *args)


def exchange(blocks, axes):
    return lax.all_to_all(blocks, axes, 0, 0, tiled=True)


def gather(own, axes, count):
    return exchange(jnp.broadcast_to(own[None], (count,) + own.shape), axes)


def around_x(block, shift):
    return lax.ppermute(block, "x", [(x, (x + shift) % 4) for x in range(4)])


def along_zl(block, shift):
    return lax.ppermute(block, "zl", [(z, z + shift) for z in range(4) if 0 <= z + shift < 4])


def swap_zl(block, bit):
    return lax.ppermute(block, "zl", [(z, z ^ bit) for z in range(4)])


def total_of(parts):
    terms = [parts[i].astype(F32) for i in range(len(parts))]
    while len(terms) > 1:
        terms = [terms[i] + terms[i + 1] for i in range(0, len(terms), 2)]
    return terms[0]


def per_device(queries, resp_keys, resp_values, prompt_keys, prompt_values, cotangent, lengths):
    place = jnp.stack([lax.axis_index("zl"), lax.axis_index("x"), lengths[0]]).astype(jnp.int32)
    queries = queries[0]
    cotangent = cotangent[0]

    own_prompt = jnp.concatenate([prompt_keys, prompt_values], 1)
    own_resp = jnp.concatenate([resp_keys[0], resp_values[0]], 1)
    far = gather(own_prompt, "zh", 4).reshape(PROMPT // 8, WIDE)
    below = [along_zl(own_resp, k) for k in (1, 2, 3)]
    far, *below = lax.optimization_barrier((far, *below))

    pkv = gather(far, NEAR, 8).reshape(PROMPT, WIDE)
    column = jnp.concatenate([own_resp] + below, 0)
    rkv = [column] + [around_x(column, k) for k in (1, 2, 3)]

    forward = call(
        prompt_forward_kernel,
        [],
        [queries, pkv],
        [((PROMPT, ROWS), BF16), ((8, ROWS), F32), ((8, ROWS), F32), ((HEAD, ROWS), F32)],
        [((ROWS, HEAD), BF16), ((PROMPT, ROWS), F32)],
        2,
        PROMPT,
    )
    out, pgrad, dq_prompt, cols, delta, peak = call(
        middle_kernel,
        [place],
        [queries, cotangent, pkv] + rkv + list(forward),
        [((BLOCK, ROWS), BF16), ((PROMPT, WIDE), BF16), ((HEAD, ROWS), F32), ((HEAD, ROWS), BF16),
         ((1, ROWS), F32), ((1, ROWS), F32)],
        [((ROWS, HEAD), BF16), ((ROWS, HEAD), BF16), ((HEAD, ROWS), BF16), ((1, ROWS), F32),
         ((LEN, ROWS), F32), ((8, ROWS), F32), ((8, ROWS), F32), ((HEAD, ROWS), F32)],
        6,
        PROMPT,
    )
    dq, rgrad = call(
        resp_backward_kernel,
        [place],
        [queries] + rkv + [cols, delta, peak, dq_prompt],
        [((BLOCK, ROWS), BF16), ((4, LEN // 4, WIDE), BF16)],
        [((ROWS, HEAD), BF16), ((ROWS, HEAD), BF16), ((HEAD, ROWS), F32)],
        5,
        LEN,
    )

    near, _ = lax.optimization_barrier((exchange(pgrad.reshape(8, PROMPT // 8, WIDE), NEAR), rgrad))
    part = total_of(near).astype(BF16)
    part = exchange(part.reshape(4, PROMPT // 32, WIDE), "zh")

    column = total_of([rgrad[0]] + [around_x(rgrad[k], k) for k in (1, 2, 3)])
    sent = column.astype(BF16)
    down = [along_zl(sent[k * BLOCK:(k + 1) * BLOCK], -k) for k in (1, 2, 3)]
    part, *down = lax.optimization_barrier((part, *down))
    grad_resp = total_of([column[:BLOCK]] + down)

    part = total_of(part).astype(BF16)
    ring = [part] + [around_x(part, k) for k in (1, 2, 3)]
    part = total_of([ring[0], ring[2], ring[1], ring[3]]).astype(BF16)
    part = total_of([part, swap_zl(part, 1)]).astype(BF16)
    grad_prompt = total_of([part, swap_zl(part, 2)])
    return (
        out[None],
        dq[None],
        grad_resp[None, :, :HEAD],
        grad_resp[None, :, HEAD:],
        grad_prompt[:, :HEAD],
        grad_prompt[:, HEAD:],
    )


def solution(mesh):
    fine = jax.sharding.Mesh(mesh.devices.reshape(4, 4, 2, 4, 4), AXES)
    rows = P(CTX, RESP, None)
    return jax.shard_map(
        per_device,
        mesh=fine,
        in_specs=(rows, rows, rows, P(CTX, None), P(CTX, None), rows, P(CTX)),
        out_specs=(rows, rows, rows, rows, P(CTX, None), P(CTX, None)),
        check_vma=False,
    )
```

time: 151 us -> 143 us (0.947)
  the two profiles are of different devices: /device:TPU:40 before, /device:TPU:46 now
where the time goes in v2:
time: 143 us; the launch traced here: 142 us
  starting transfers between devices  81.3 us (57%)
  waiting for transfers between devices  34.1 us (24%)
  Pallas kernels  17.4 us (12%)
  other arithmetic  4.74 us (3%)
  local copies, waits for them, and re-layouts  3.08 us (2%)
  between operations  1.53 us (1%)
    all_to_all x4, starting transfers between devices, exchange(): return lax.all_to_all(blocks, axes, 0, 0, tiled=True)  33 us
    ppermute x9, starting transfers between devices, around_x(): return lax.ppermute(block, 'x', [(x, (x + shift) % 4) for x in range(4)])  29.7 us
    ppermute x6, waiting for transfers between devices, along_zl(): lax.ppermute(block, 'zl', [(z, z + shift) for z in range(4) if 0 <= z + s...  17.7 us
    pallas_call x3, Pallas kernels, call(): pl.pallas_call(kernel, out_shape=tuple((jax.ShapeDtypeStruct(shape, dtype...  17.4 us
    ppermute x6, starting transfers between devices, along_zl(): lax.ppermute(block, 'zl', [(z, z + shift) for z in range(4) if 0 <= z + s...  10.5 us
    ppermute x2, starting transfers between devices, swap_zl(): return lax.ppermute(block, 'zl', [(z, z ^ bit) for z in range(4)])  8.1 us
    ppermute x9, waiting for transfers between devices, around_x(): return lax.ppermute(block, 'x', [(x, (x + shift) % 4) for x in range(4)])  6.97 us
    ppermute x2, waiting for transfers between devices, swap_zl(): return lax.ppermute(block, 'zl', [(z, z ^ bit) for z in range(4)])  5.06 us
  transfers between devices with their start and end apart: 21, of which 13 were waited for; matrix products, arithmetic and copies ran while one was open for 3% of the time, Pallas kernels for 6%

profile of v2, /device:TPU:46, one launch (start us, length us, event | category | flops | bytes accessed | tf_op | source)
XLA Modules:
  0.0 142.1 jit_solution(7376313471680731702)
XLA Ops:
  2.1 14.2 %all-to-all-start = ((bf16[4,64,256]{2,1,0:T(8,128)(2,1)}), bf16[4,64,256]{2,1,0:T(8,128)(2,1)S(1)}, u32[]{:S(2)}, u32[]{:S(2)}) async-start(bf16[4,64,256]{2,1,0:T(8,128)(2,1)} %broadcast_in_dim.24), calls=%async_computation | async-start | bytes 262144 | tf_op jit(solution)/shard_map/all_to_all | solution.py:214
  17.7 4.0 %collective-permute-start.1 = (bf16[128,256]{1,0:T(8,128)(2,1)S(1)}, bf16[128,256]{1,0:T(8,128)(2,1)S(1)}, u32[]{:S(2)}, u32[]{:S(2)}) collective-permute-start(bf16[128,256]{1,0:T(8,128)(2,1)S(1)} %pad_maximum_fusion.1), channel_id=1, source_target_pairs={{0,8},{4,12},{1,9},{5,13},{2,10},{6,14},{3,11},{7,15},{16,24},{20,... | collective-permute-start | bytes 196616 | tf_op jit(solution)/shard_map/ppermute | solution.py:226
  21.7 1.9 %collective-permute-start = (bf16[128,256]{1,0:T(8,128)(2,1)S(1)}, bf16[128,256]{1,0:T(8,128)(2,1)S(1)}, u32[]{:S(2)}, u32[]{:S(2)}) collective-permute-start(bf16[128,256]{1,0:T(8,128)(2,1)S(1)} %pad_maximum_fusion.1), channel_id=1, source_target_pairs={{0,4},{4,8},{8,12},{1,5},{5,9},{9,13},{2,6},{6,10},{10,14},{3,7},{... | collective-permute-start | bytes 196616 | tf_op jit(solution)/shard_map/ppermute | solution.py:226
  23.7 4.6 %collective-permute-done.1 = bf16[128,256]{1,0:T(8,128)(2,1)S(1)} collective-permute-done((bf16[128,256]{1,0:T(8,128)(2,1)S(1)}, bf16[128,256]{1,0:T(8,128)(2,1)S(1)}, u32[]{:S(2)}, u32[]{:S(2)}) %collective-permute-start.1) | collective-permute-done | bytes 65568 | tf_op jit(solution)/shard_map/ppermute | solution.py:226
  31.8 4.9 %all-to-all-start.1 = ((bf16[8,256,256]{2,1,0:T(8,128)(2,1)}), bf16[8,256,256]{2,1,0:T(8,128)(2,1)S(1)}, u32[]{:S(2)}, u32[]{:S(2)}) async-start(bf16[8,256,256]{2,1,0:T(8,128)(2,1)} %broadcast_in_dim.25), calls=%async_computation.1 | async-start | bytes 2097152 | tf_op jit(solution)/shard_map/all_to_all | solution.py:214
  37.6 2.7 %collective-permute-start.5 = (bf16[512,256]{1,0:T(8,128)(2,1)S(1)}, bf16[512,256]{1,0:T(8,128)(2,1)S(1)}, u32[]{:S(2)}, u32[]{:S(2)}) collective-permute-start(bf16[512,256]{1,0:T(8,128)(2,1)S(1)} %pad_maximum_fusion.r0), channel_id=1, source_target_pairs={{0,3},{1,0},{2,1},{3,2},{4,7},{5,4},{6,5},{7,6},{8,11},{9,8},{10,9... | collective-permute-start | bytes 786440 | tf_op jit(solution)/shard_map/ppermute | solution.py:222
  40.3 3.0 %collective-permute-start.4 = (bf16[512,256]{1,0:T(8,128)(2,1)S(1)}, bf16[512,256]{1,0:T(8,128)(2,1)S(1)}, u32[]{:S(2)}, u32[]{:S(2)}) collective-permute-start(bf16[512,256]{1,0:T(8,128)(2,1)S(1)} %pad_maximum_fusion.r0), channel_id=1, source_target_pairs={{0,2},{1,3},{2,0},{3,1},{4,6},{5,7},{6,4},{7,5},{8,10},{9,11},{10,... | collective-permute-start | bytes 786440 | tf_op jit(solution)/shard_map/ppermute | solution.py:222
  43.3 4.0 %collective-permute-start.3 = (bf16[512,256]{1,0:T(8,128)(2,1)S(1)}, bf16[512,256]{1,0:T(8,128)(2,1)S(1)}, u32[]{:S(2)}, u32[]{:S(2)}) collective-permute-start(bf16[512,256]{1,0:T(8,128)(2,1)S(1)} %pad_maximum_fusion.r0), channel_id=1, source_target_pairs={{0,1},{1,2},{2,3},{3,0},{4,5},{5,6},{6,7},{7,4},{8,9},{9,10},{10,1... | collective-permute-start | bytes 786440 | tf_op jit(solution)/shard_map/ppermute | solution.py:222
  48.1 3.2 %all-to-all-done.1 = bf16[8,256,256]{2,1,0:T(8,128)(2,1)S(1)} async-done(((bf16[8,256,256]{2,1,0:T(8,128)(2,1)}), bf16[8,256,256]{2,1,0:T(8,128)(2,1)S(1)}, u32[]{:S(2)}, u32[]{:S(2)}) %all-to-all-start.1) | async-done | bytes 1048608 | tf_op jit(solution)/shard_map/all_to_all | solution.py:214
  51.3 4.1 %shard_map.118 = (bf16[2048,1024]{1,0:T(8,128)(2,1)S(1)}, f32[8,1024]{1,0:T(8,128)S(1)}, f32[8,1024]{1,0:T(8,128)S(1)}, f32[128,1024]{1,0:T(8,128)S(1)}) custom-call(bf16[128,1024]{1,0:T(8,128)(2,1)S(1)} %bitcast.33, bf16[2048,256]{1,0:T(8,128)(2,1)S(1)} %bitcast.30), custom_call_target="tpu_custom_call" | custom-call | flops 1073741824 | bytes 6291456 | tf_op jit(solution)/shard_map/pallas_call | solution.py:198
  57.2 8.7 %shard_map.119 = (bf16[128,1024]{1,0:T(8,128)(2,1)}, bf16[2048,256]{1,0:T(8,128)(2,1)}, f32[128,1024]{1,0:T(8,128)S(1)}, bf16[128,1024]{1,0:T(8,128)(2,1)S(1)}, ...) custom-call(s32[3]{0:T(128)S(1)} %pad_add_fusion.place, bf16[128,1024]{1,0:T(8,128)(2,1)S(1)} %bitcast.34, ...), custom_call_target="tpu_custom_call" | custom-call | flops 3221225472 | bytes 6291456 | tf_op jit(solution)/shard_map/pallas_call | solution.py:198
  65.9 4.8 %all-to-all-start.2 = ((bf16[8,256,256]{2,1,0:T(8,128)(2,1)}), bf16[8,256,256]{2,1,0:T(8,128)(2,1)}, u32[]{:S(2)}, u32[]{:S(2)}) async-start(bf16[8,256,256]{2,1,0:T(8,128)(2,1)} %bitcast.14), calls=%async_computation.2 | async-start | bytes 2097152 | tf_op jit(solution)/shard_map/all_to_all | solution.py:214
  70.7 4.6 %shard_map.120 = (bf16[128,1024]{1,0:T(8,128)(2,1)}, bf16[4,512,256]{2,1,0:T(8,128)(2,1)S(1)}) custom-call(s32[3]{0:T(128)S(1)} %pad_add_fusion.place, bf16[128,1024]{1,0:T(8,128)(2,1)S(1)} %bitcast.35, bf16[512,256]{1,0:T(8,128)(2,1)S(1)} %pad_maximum_fusion.r0, bf16[512,256]{1,0:T(8,128)(2,1)S(1)} %collective-permute-done.3.r1, ...), custom_call_target="tpu_custom_call" | custom-call | flops 2684354560 | bytes 6291456 | tf_op jit(solution)/shard_map/pallas_call | solution.py:198
  75.3 4.5 %collective-permute-start.6 = (bf16[512,256]{1,0:T(8,128)(2,1)S(1)}, bf16[512,256]{1,0:T(8,128)(2,1)S(1)}, u32[]{:S(2)}, u32[]{:S(2)}) collective-permute-start(bf16[512,256]{1,0:T(8,128)(2,1)S(1)} %get-tuple-element.50), channel_id=1, source_target_pairs={{0,1},{1,2},{2,3},{3,0},{4,5},{5,6},{6,7},{7,4},{8,9},{9,10},{10,1... | collective-permute-start | bytes 786440 | tf_op jit(solution)/shard_map/ppermute | solution.py:222
  79.8 1.9 %collective-permute-start.8 = (bf16[512,256]{1,0:T(8,128)(2,1)S(1)}, bf16[512,256]{1,0:T(8,128)(2,1)S(1)}, u32[]{:S(2)}, u32[]{:S(2)}) collective-permute-start(bf16[512,256]{1,0:T(8,128)(2,1)S(1)} %get-tuple-element.51), channel_id=1, source_target_pairs={{0,3},{1,0},{2,1},{3,2},{4,7},{5,4},{6,5},{7,6},{8,11},{9,8},{10,9... | collective-permute-start | bytes 786440 | tf_op jit(solution)/shard_map/ppermute | solution.py:222
  81.8 3.4 %collective-permute-start.7 = (bf16[512,256]{1,0:T(8,128)(2,1)S(1)}, bf16[512,256]{1,0:T(8,128)(2,1)S(1)}, u32[]{:S(2)}, u32[]{:S(2)}) collective-permute-start(bf16[512,256]{1,0:T(8,128)(2,1)S(1)} %get-tuple-element.52), channel_id=1, source_target_pairs={{0,2},{1,3},{2,0},{3,1},{4,6},{5,7},{6,4},{7,5},{8,10},{9,11},{10,... | collective-permute-start | bytes 786440 | tf_op jit(solution)/shard_map/ppermute | solution.py:222
  85.3 2.1 %add_convert_fusion = bf16[1,256,256]{2,1,0:T(8,128)(2,1)} fusion(bf16[8,256,256]{2,1,0:T(8,128)(2,1)} %all-to-all-done.2), kind=kLoop, calls=%fused_computation.3 | loop fusion | flops 1048576 | bytes 1179648 | tf_op jit(solution)/shard_map/convert.1
  87.4 9.1 %all-to-all-start.3 = ((bf16[4,64,256]{2,1,0:T(8,128)(2,1)}), bf16[4,64,256]{2,1,0:T(8,128)(2,1)S(1)}, u32[]{:S(2)}, u32[]{:S(2)}) async-start(bf16[4,64,256]{2,1,0:T(8,128)(2,1)} %bitcast.15), calls=%async_computation.3 | async-start | bytes 262144 | tf_op jit(solution)/shard_map/all_to_all | solution.py:214
  100.7 9.9 %collective-permute-done.10 = bf16[128,256]{1,0:T(8,128)(2,1)S(1)} collective-permute-done((bf16[128,256]{1,0:T(8,128)(2,1)S(1)}, bf16[128,256]{1,0:T(8,128)(2,1)S(1)}, u32[]{:S(2)}, u32[]{:S(2)}) %collective-permute-start.10) | collective-permute-done | bytes 65568 | tf_op jit(solution)/shard_map/ppermute | solution.py:226
  112.3 3.7 %collective-permute-start.13 = (bf16[64,256]{1,0:T(8,128)(2,1)S(1)}, bf16[64,256]{1,0:T(8,128)(2,1)S(1)}, u32[]{:S(2)}, u32[]{:S(2)}) collective-permute-start(bf16[64,256]{1,0:T(8,128)(2,1)S(1)} %fusion.2), channel_id=1, source_target_pairs={{0,1},{1,2},{2,3},{3,0},{4,5},{5,6},{6,7},{7,4},{8,9},{9,10},{10,1... | collective-permute-start | bytes 98312 | tf_op jit(solution)/shard_map/ppermute | solution.py:222
  116.1 4.4 %collective-permute-start.12 = (bf16[64,256]{1,0:T(8,128)(2,1)S(1)}, bf16[64,256]{1,0:T(8,128)(2,1)S(1)}, u32[]{:S(2)}, u32[]{:S(2)}) collective-permute-start(bf16[64,256]{1,0:T(8,128)(2,1)S(1)} %fusion.2), channel_id=1, source_target_pairs={{0,2},{1,3},{2,0},{3,1},{4,6},{5,7},{6,4},{7,5},{8,10},{9,11},{10,... | collective-permute-start | bytes 98312 | tf_op jit(solution)/shard_map/ppermute | solution.py:222
  123.4 4.1 %collective-permute-done.14 = bf16[64,256]{1,0:T(8,128)(2,1)S(1)} collective-permute-done((bf16[64,256]{1,0:T(8,128)(2,1)S(1)}, bf16[64,256]{1,0:T(8,128)(2,1)S(1)}, u32[]{:S(2)}, u32[]{:S(2)}) %collective-permute-start.14) | collective-permute-done | bytes 32800 | tf_op jit(solution)/shard_map/ppermute | solution.py:222
  129.5 3.8 %collective-permute-done.15 = bf16[64,256]{1,0:T(8,128)(2,1)S(1)} collective-permute-done((bf16[64,256]{1,0:T(8,128)(2,1)S(1)}, bf16[64,256]{1,0:T(8,128)(2,1)S(1)}, u32[]{:S(2)}, u32[]{:S(2)}) %collective-permute-start.15) | collective-permute-done | bytes 32800 | tf_op jit(solution)/shard_map/ppermute | solution.py:230
  133.4 6.2 %collective-permute-start.16 = (bf16[64,256]{1,0:T(8,128)(2,1)S(1)}, bf16[64,256]{1,0:T(8,128)(2,1)S(1)}, u32[]{:S(2)}, u32[]{:S(2)}) collective-permute-start(bf16[64,256]{1,0:T(8,128)(2,1)S(1)} %add_convert_fusion.1), channel_id=1, source_target_pairs={{0,8},{4,12},{8,0},{12,4},{1,9},{5,13},{9,1},{13,5},{2,10},{6,14},... | collective-permute-start | bytes 98312 | tf_op jit(solution)/shard_map/ppermute | solution.py:230
  (42 shorter events, 22.5 us)
Async XLA Ops:
  0.6 50.6 %copy-start.1 = (bf16[1,128,1024]{2,1,0:T(8,128)(2,1)S(1)}, bf16[1,128,1024]{2,1,0:T(8,128)(2,1)}, u32[]{:S(2)}) copy-start(bf16[1,128,1024]{2,1,0:T(8,128)(2,1)} %param.7) | copy-start | bytes 786436
  1.4 55.8 %copy-start = (bf16[1,128,1024]{2,1,0:T(8,128)(2,1)S(1)}, bf16[1,128,1024]{2,1,0:T(8,128)(2,1)}, u32[]{:S(2)}) copy-start(bf16[1,128,1024]{2,1,0:T(8,128)(2,1)} %param.12) | copy-start | bytes 786436
  2.1 28.7 %all-to-all-start = ((bf16[4,64,256]{2,1,0:T(8,128)(2,1)}), bf16[4,64,256]{2,1,0:T(8,128)(2,1)S(1)}, u32[]{:S(2)}, u32[]{:S(2)}) async-start(bf16[4,64,256]{2,1,0:T(8,128)(2,1)} %broadcast_in_dim.24), calls=%async_computation | async-start | bytes 262144 | tf_op jit(solution)/shard_map/all_to_all | solution.py:214
  17.1 6.6 %collective-permute-start.2 = (bf16[128,256]{1,0:T(8,128)(2,1)S(1)}, bf16[128,256]{1,0:T(8,128)(2,1)S(1)}, u32[]{:S(2)}, u32[]{:S(2)}) collective-permute-start(bf16[128,256]{1,0:T(8,128)(2,1)S(1)} %pad_maximum_fusion.1), channel_id=1, source_target_pairs={{0,12},{1,13},{2,14},{3,15},{16,28},{17,29},{18,30},{19,31},{32,44... | collective-permute-start | bytes 196616 | tf_op jit(solution)/shard_map/ppermute | solution.py:226
  17.7 10.5 %collective-permute-start.1 = (bf16[128,256]{1,0:T(8,128)(2,1)S(1)}, bf16[128,256]{1,0:T(8,128)(2,1)S(1)}, u32[]{:S(2)}, u32[]{:S(2)}) collective-permute-start(bf16[128,256]{1,0:T(8,128)(2,1)S(1)} %pad_maximum_fusion.1), channel_id=1, source_target_pairs={{0,8},{4,12},{1,9},{5,13},{2,10},{6,14},{3,11},{7,15},{16,24},{20,... | collective-permute-start | bytes 196616 | tf_op jit(solution)/shard_map/ppermute | solution.py:226
  21.7 8.1 %collective-permute-start = (bf16[128,256]{1,0:T(8,128)(2,1)S(1)}, bf16[128,256]{1,0:T(8,128)(2,1)S(1)}, u32[]{:S(2)}, u32[]{:S(2)}) collective-permute-start(bf16[128,256]{1,0:T(8,128)(2,1)S(1)} %pad_maximum_fusion.1), channel_id=1, source_target_pairs={{0,4},{4,8},{8,12},{1,5},{5,9},{9,13},{2,6},{6,10},{10,14},{3,7},{... | collective-permute-start | bytes 196616 | tf_op jit(solution)/shard_map/ppermute | solution.py:226
  31.8 19.4 %all-to-all-start.1 = ((bf16[8,256,256]{2,1,0:T(8,128)(2,1)}), bf16[8,256,256]{2,1,0:T(8,128)(2,1)S(1)}, u32[]{:S(2)}, u32[]{:S(2)}) async-start(bf16[8,256,256]{2,1,0:T(8,128)(2,1)} %broadcast_in_dim.25), calls=%async_computation.1 | async-start | bytes 2097152 | tf_op jit(solution)/shard_map/all_to_all | solution.py:214
  37.6 17.9 %collective-permute-start.5 = (bf16[512,256]{1,0:T(8,128)(2,1)S(1)}, bf16[512,256]{1,0:T(8,128)(2,1)S(1)}, u32[]{:S(2)}, u32[]{:S(2)}) collective-permute-start(bf16[512,256]{1,0:T(8,128)(2,1)S(1)} %pad_maximum_fusion.r0), channel_id=1, source_target_pairs={{0,3},{1,0},{2,1},{3,2},{4,7},{5,4},{6,5},{7,6},{8,11},{9,8},{10,9... | collective-permute-start | bytes 786440 | tf_op jit(solution)/shard_map/ppermute | solution.py:222
  40.3 15.1 %collective-permute-start.4 = (bf16[512,256]{1,0:T(8,128)(2,1)S(1)}, bf16[512,256]{1,0:T(8,128)(2,1)S(1)}, u32[]{:S(2)}, u32[]{:S(2)}) collective-permute-start(bf16[512,256]{1,0:T(8,128)(2,1)S(1)} %pad_maximum_fusion.r0), channel_id=1, source_target_pairs={{0,2},{1,3},{2,0},{3,1},{4,6},{5,7},{6,4},{7,5},{8,10},{9,11},{10,... | collective-permute-start | bytes 786440 | tf_op jit(solution)/shard_map/ppermute | solution.py:222
  43.3 13.8 %collective-permute-start.3 = (bf16[512,256]{1,0:T(8,128)(2,1)S(1)}, bf16[512,256]{1,0:T(8,128)(2,1)S(1)}, u32[]{:S(2)}, u32[]{:S(2)}) collective-permute-start(bf16[512,256]{1,0:T(8,128)(2,1)S(1)} %pad_maximum_fusion.r0), channel_id=1, source_target_pairs={{0,1},{1,2},{2,3},{3,0},{4,5},{5,6},{6,7},{7,4},{8,9},{9,10},{10,1... | collective-permute-start | bytes 786440 | tf_op jit(solution)/shard_map/ppermute | solution.py:222
  65.9 19.4 %all-to-all-start.2 = ((bf16[8,256,256]{2,1,0:T(8,128)(2,1)}), bf16[8,256,256]{2,1,0:T(8,128)(2,1)}, u32[]{:S(2)}, u32[]{:S(2)}) async-start(bf16[8,256,256]{2,1,0:T(8,128)(2,1)} %bitcast.14), calls=%async_computation.2 | async-start | bytes 2097152 | tf_op jit(solution)/shard_map/all_to_all | solution.py:214
  75.3 21.2 %collective-permute-start.6 = (bf16[512,256]{1,0:T(8,128)(2,1)S(1)}, bf16[512,256]{1,0:T(8,128)(2,1)S(1)}, u32[]{:S(2)}, u32[]{:S(2)}) collective-permute-start(bf16[512,256]{1,0:T(8,128)(2,1)S(1)} %get-tuple-element.50), channel_id=1, source_target_pairs={{0,1},{1,2},{2,3},{3,0},{4,5},{5,6},{6,7},{7,4},{8,9},{9,10},{10,1... | collective-permute-start | bytes 786440 | tf_op jit(solution)/shard_map/ppermute | solution.py:222
  79.8 16.8 %collective-permute-start.8 = (bf16[512,256]{1,0:T(8,128)(2,1)S(1)}, bf16[512,256]{1,0:T(8,128)(2,1)S(1)}, u32[]{:S(2)}, u32[]{:S(2)}) collective-permute-start(bf16[512,256]{1,0:T(8,128)(2,1)S(1)} %get-tuple-element.51), channel_id=1, source_target_pairs={{0,3},{1,0},{2,1},{3,2},{4,7},{5,4},{6,5},{7,6},{8,11},{9,8},{10,9... | collective-permute-start | bytes 786440 | tf_op jit(solution)/shard_map/ppermute | solution.py:222
  81.8 14.9 %collective-permute-start.7 = (bf16[512,256]{1,0:T(8,128)(2,1)S(1)}, bf16[512,256]{1,0:T(8,128)(2,1)S(1)}, u32[]{:S(2)}, u32[]{:S(2)}) collective-permute-start(bf16[512,256]{1,0:T(8,128)(2,1)S(1)} %get-tuple-element.52), channel_id=1, source_target_pairs={{0,2},{1,3},{2,0},{3,1},{4,6},{5,7},{6,4},{7,5},{8,10},{9,11},{10,... | collective-permute-start | bytes 786440 | tf_op jit(solution)/shard_map/ppermute | solution.py:222
  87.4 24.9 %all-to-all-start.3 = ((bf16[4,64,256]{2,1,0:T(8,128)(2,1)}), bf16[4,64,256]{2,1,0:T(8,128)(2,1)S(1)}, u32[]{:S(2)}, u32[]{:S(2)}) async-start(bf16[4,64,256]{2,1,0:T(8,128)(2,1)} %bitcast.15), calls=%async_computation.3 | async-start | bytes 262144 | tf_op jit(solution)/shard_map/all_to_all | solution.py:214
  96.8 3.9 %collective-permute-start.11 = (bf16[128,256]{1,0:T(8,128)(2,1)S(1)}, bf16[128,256]{1,0:T(8,128)(2,1)S(1)}, u32[]{:S(2)}, u32[]{:S(2)}) collective-permute-start(bf16[128,256]{1,0:T(8,128)(2,1)S(1)} %get-tuple-element.53), channel_id=1, source_target_pairs={{12,0},{13,1},{14,2},{15,3},{28,16},{29,17},{30,18},{31,19},{44,32... | collective-permute-start | bytes 196616 | tf_op jit(solution)/shard_map/ppermute | solution.py:226
  97.5 13.2 %collective-permute-start.10 = (bf16[128,256]{1,0:T(8,128)(2,1)S(1)}, bf16[128,256]{1,0:T(8,128)(2,1)S(1)}, u32[]{:S(2)}, u32[]{:S(2)}) collective-permute-start(bf16[128,256]{1,0:T(8,128)(2,1)S(1)} %get-tuple-element.54), channel_id=1, source_target_pairs={{8,0},{12,4},{9,1},{13,5},{10,2},{14,6},{11,3},{15,7},{24,16},{28,... | collective-permute-start | bytes 196616 | tf_op jit(solution)/shard_map/ppermute | solution.py:226
  98.8 13.5 %collective-permute-start.9 = (bf16[128,256]{1,0:T(8,128)(2,1)S(1)}, bf16[128,256]{1,0:T(8,128)(2,1)S(1)}, u32[]{:S(2)}, u32[]{:S(2)}) collective-permute-start(bf16[128,256]{1,0:T(8,128)(2,1)S(1)} %get-tuple-element.55), channel_id=1, source_target_pairs={{4,0},{8,4},{12,8},{5,1},{9,5},{13,9},{6,2},{10,6},{14,10},{7,3},{... | collective-permute-start | bytes 196616 | tf_op jit(solution)/shard_map/ppermute | solution.py:226
  112.3 10.1 %collective-permute-start.13 = (bf16[64,256]{1,0:T(8,128)(2,1)S(1)}, bf16[64,256]{1,0:T(8,128)(2,1)S(1)}, u32[]{:S(2)}, u32[]{:S(2)}) collective-permute-start(bf16[64,256]{1,0:T(8,128)(2,1)S(1)} %fusion.2), channel_id=1, source_target_pairs={{0,1},{1,2},{2,3},{3,0},{4,5},{5,6},{6,7},{7,4},{8,9},{9,10},{10,1... | collective-permute-start | bytes 98312 | tf_op jit(solution)/shard_map/ppermute | solution.py:222
  116.1 7.3 %collective-permute-start.12 = (bf16[64,256]{1,0:T(8,128)(2,1)S(1)}, bf16[64,256]{1,0:T(8,128)(2,1)S(1)}, u32[]{:S(2)}, u32[]{:S(2)}) collective-permute-start(bf16[64,256]{1,0:T(8,128)(2,1)S(1)} %fusion.2), channel_id=1, source_target_pairs={{0,2},{1,3},{2,0},{3,1},{4,6},{5,7},{6,4},{7,5},{8,10},{9,11},{10,... | collective-permute-start | bytes 98312 | tf_op jit(solution)/shard_map/ppermute | solution.py:222
  120.5 7.0 %collective-permute-start.14 = (bf16[64,256]{1,0:T(8,128)(2,1)S(1)}, bf16[64,256]{1,0:T(8,128)(2,1)S(1)}, u32[]{:S(2)}, u32[]{:S(2)}) collective-permute-start(bf16[64,256]{1,0:T(8,128)(2,1)S(1)} %fusion.2), channel_id=1, source_target_pairs={{0,3},{1,0},{2,1},{3,2},{4,7},{5,4},{6,5},{7,6},{8,11},{9,8},{10,9... | collective-permute-start | bytes 98312 | tf_op jit(solution)/shard_map/ppermute | solution.py:222
  127.6 5.8 %collective-permute-start.15 = (bf16[64,256]{1,0:T(8,128)(2,1)S(1)}, bf16[64,256]{1,0:T(8,128)(2,1)S(1)}, u32[]{:S(2)}, u32[]{:S(2)}) collective-permute-start(bf16[64,256]{1,0:T(8,128)(2,1)S(1)} %add_convert_fusion.2), channel_id=1, source_target_pairs={{0,4},{4,0},{8,12},{12,8},{1,5},{5,1},{9,13},{13,9},{2,6},{6,2},{1... | collective-permute-start | bytes 98312 | tf_op jit(solution)/shard_map/ppermute | solution.py:230
  133.4 8.1 %collective-permute-start.16 = (bf16[64,256]{1,0:T(8,128)(2,1)S(1)}, bf16[64,256]{1,0:T(8,128)(2,1)S(1)}, u32[]{:S(2)}, u32[]{:S(2)}) collective-permute-start(bf16[64,256]{1,0:T(8,128)(2,1)S(1)} %add_convert_fusion.1), channel_id=1, source_target_pairs={{0,8},{4,12},{8,0},{12,4},{1,9},{5,13},{9,1},{13,5},{2,10},{6,14},... | collective-permute-start | bytes 98312 | tf_op jit(solution)/shard_map/ppermute | solution.py:230

commit v3 on v2

--- a/solution.py
+++ b/solution.py
@@ -14,6 +14,7 @@
 CHUNK = 512
 PROMPT = 2048
 LEN = 2048
+PIECE = 16
 WIDE = 2 * HEAD
 SCALE = 1.0 / math.sqrt(HEAD)
 EXP2_SCALE = SCALE * math.log2(math.e)
@@ -50,15 +51,48 @@
     return pl.ds(pl.multiple_of(i * CHUNK, CHUNK), CHUNK)
 
 
-def masked_scores(keys, q_rows, x):
-    s = scores_of(keys, q_rows)
-    row = lax.broadcasted_iota(jnp.int32, (CHUNK, ROWS), 0)
-    key_pos = ((x - row // BLOCK) & 3) * BLOCK + row % BLOCK
-    query_pos = x * BLOCK + lax.broadcasted_iota(jnp.int32, (CHUNK, ROWS), 1) % BLOCK
-    return jnp.where(key_pos <= query_pos, s, -1e30)
-
-
-def prompt_forward_kernel(q_ref, pkv_ref, e_ref, top_ref, total_ref, acc_ref, q_rows, s_all):
+def bias_of(key_pos, x):
+    query_pos = x * BLOCK + lax.broadcasted_iota(jnp.int32, (CHUNK, BLOCK), 1)
+    return jnp.where(key_pos <= query_pos, 0.0, -1e30).astype(F32)
+
+
+def chunk_rows():
+    row = lax.broadcasted_iota(jnp.int32, (CHUNK, BLOCK), 0)
+    return row // BLOCK, row % BLOCK
+
+
+def level_bias(x):
+    slot, row = chunk_rows()
+    return bias_of(((x - slot) & 3) * BLOCK + row, x)
+
+
+def column_bias(zl, x, i):
+    slot, row = chunk_rows()
+    key_pos = (((x - i) & 3) - 4 * slot) * BLOCK + row
+    return bias_of(jnp.where(slot <= zl, key_pos, LEN), x)
+
+
+def biased(s, bias):
+    return s + jnp.concatenate([bias] * HEADS, 1)
+
+
+def column_scores(columns, zl, x, q_rows, s_all, start, top):
+    for n, (ref, i) in enumerate(columns):
+        s = biased(scores_of(ref[:, 0:HEAD], q_rows), column_bias(zl, x, i))
+        s_all[start + n * CHUNK:start + (n + 1) * CHUNK, :] = s
+        top[...] = jnp.maximum(top[...], fold(jnp.max, s))
+
+
+def column_weights(columns, peak, s_all, start, total, acc):
+    for n, (ref, i) in enumerate(columns):
+        e = jnp.exp2((s_all[start + n * CHUNK:start + (n + 1) * CHUNK, :] - peak) * EXP2_SCALE)
+        total[...] += fold(jnp.sum, e)
+        acc[...] += jnp.dot(ref[:, HEAD:WIDE].T, e.astype(BF16), preferred_element_type=F32)
+
+
+def prompt_forward_kernel(place, q_ref, pkv_ref, r0, r3, e_ref, top_ref, total_ref, acc_ref, q_rows, s_all):
+    zl, x = place[0], place[1]
+    columns = ((r0, 0), (r3, 3))
     load_rows(q_rows, q_ref)
     top_ref[...] = jnp.full(top_ref.shape, -1e30, F32)
 
@@ -69,6 +103,7 @@
         return carry
 
     lax.fori_loop(0, PROMPT // CHUNK, score_step, 0)
+    column_scores(columns, zl, x, q_rows, s_all, PROMPT, top_ref)
     peak = jnp.max(top_ref[...], 0, keepdims=True)
     total_ref[...] = jnp.zeros(total_ref.shape, F32)
     acc_ref[...] = jnp.zeros(acc_ref.shape, F32)
@@ -82,40 +117,25 @@
         return carry
 
     lax.fori_loop(0, PROMPT // CHUNK, weight_step, 0)
-
-
-def middle_kernel(place, q_ref, c_ref, pkv_ref, r0, r1, r2, r3, e_ref, ptop_ref, ptotal_ref, pacc_ref,
+    column_weights(columns, peak, s_all, PROMPT, total_ref, acc_ref)
+
+
+def middle_kernel(place, q_ref, c_ref, pkv_ref, r1, r2, e_ref, ptop_ref, ptotal_ref, pacc_ref,
                   out_ref, pg_ref, dq_ref, cols_ref, delta_ref, peak_ref,
                   q_rows, c_rows, c_cols, pdelta, s_all, top, total, acc):
-    refs = (r0, r1, r2, r3)
+    columns = ((r1, 1), (r2, 2))
     zl, x, length = place[0], place[1], place[2]
     first = (zl * 4 + x) * BLOCK
     load_rows(q_rows, q_ref)
 
-    s = masked_scores(resp_rows(refs, 0, 0), q_rows, x)
-    s_all[0:CHUNK, :] = s
-    top[...] = jnp.maximum(ptop_ref[...], fold(jnp.max, s))
-
-    def score_step(j, carry):
-        s = scores_of(resp_rows(refs, j, 0), q_rows)
-        s_all[chunk_at(j), :] = s
-        top[...] = jnp.maximum(top[...], fold(jnp.max, s))
-        return carry
-
-    lax.fori_loop(1, zl + 1, score_step, 0)
+    top[...] = ptop_ref[...]
+    column_scores(columns, zl, x, q_rows, s_all, 0, top)
     peak = jnp.max(top[...], 0, keepdims=True)
     peak_ref[...] = peak
     share = jnp.exp2((jnp.max(ptop_ref[...], 0, keepdims=True) - peak) * EXP2_SCALE)
     total[...] = ptotal_ref[...] * share
     acc[...] = pacc_ref[...] * share
-
-    def weight_step(j, carry):
-        e = jnp.exp2((s_all[chunk_at(j), :] - peak) * EXP2_SCALE)
-        total[...] += fold(jnp.sum, e)
-        acc[...] += jnp.dot(resp_rows(refs, j, HEAD).T, e.astype(BF16), preferred_element_type=F32)
-        return carry
-
-    lax.fori_loop(0, zl + 1, weight_step, 0)
+    column_weights(columns, peak, s_all, 0, total, acc)
     inverse = 1.0 / jnp.sum(total[...], 0, keepdims=True)
 
     for h in range(HEADS):
@@ -179,7 +199,7 @@
             rg_ref[(4 - i) % 4, at, HEAD:WIDE] = dv[rows]
 
     keys = resp_rows(refs, 0, 0)
-    grad_step(0, keys, masked_scores(keys, q_rows, x))
+    grad_step(0, keys, biased(scores_of(keys, q_rows), level_bias(x)))
 
     def full_step(j, carry):
         keys = resp_rows(refs, j, 0)
@@ -226,10 +246,6 @@
     return lax.ppermute(block, "zl", [(z, z + shift) for z in range(4) if 0 <= z + shift < 4])
 
 
-def swap_zl(block, bit):
-    return lax.ppermute(block, "zl", [(z, z ^ bit) for z in range(4)])
-
-
 def total_of(parts):
     terms = [parts[i].astype(F32) for i in range(len(parts))]
     while len(terms) > 1:
@@ -254,21 +270,21 @@
 
     forward = call(
         prompt_forward_kernel,
-        [],
-        [queries, pkv],
+        [place],
+        [queries, pkv, rkv[0], rkv[3]],
         [((PROMPT, ROWS), BF16), ((8, ROWS), F32), ((8, ROWS), F32), ((HEAD, ROWS), F32)],
-        [((ROWS, HEAD), BF16), ((PROMPT, ROWS), F32)],
+        [((ROWS, HEAD), BF16), ((PROMPT + 2 * CHUNK, ROWS), F32)],
         2,
-        PROMPT,
+        PROMPT + 2 * CHUNK,
     )
     out, pgrad, dq_prompt, cols, delta, peak = call(
         middle_kernel,
         [place],
-        [queries, cotangent, pkv] + rkv + list(forward),
+        [queries, cotangent, pkv, rkv[1], rkv[2]] + list(forward),
         [((BLOCK, ROWS), BF16), ((PROMPT, WIDE), BF16), ((HEAD, ROWS), F32), ((HEAD, ROWS), BF16),
          ((1, ROWS), F32), ((1, ROWS), F32)],
         [((ROWS, HEAD), BF16), ((ROWS, HEAD), BF16), ((HEAD, ROWS), BF16), ((1, ROWS), F32),
-         ((LEN, ROWS), F32), ((8, ROWS), F32), ((8, ROWS), F32), ((HEAD, ROWS), F32)],
+         ((2 * CHUNK, ROWS), F32), ((8, ROWS), F32), ((8, ROWS), F32), ((HEAD, ROWS), F32)],
         6,
         PROMPT,
     )
@@ -283,8 +299,8 @@
     )
 
     near, _ = lax.optimization_barrier((exchange(pgrad.reshape(8, PROMPT // 8, WIDE), NEAR), rgrad))
-    part = total_of(near).astype(BF16)
-    part = exchange(part.reshape(4, PROMPT // 32, WIDE), "zh")
+    part = lax.optimization_barrier(jnp.sum(near.astype(F32), 0)).astype(BF16)
+    part = exchange(part.reshape(16, PIECE, WIDE), ("zh", "zl"))
 
     column = total_of([rgrad[0]] + [around_x(rgrad[k], k) for k in (1, 2, 3)])
     sent = column.astype(BF16)
@@ -292,11 +308,8 @@
     part, *down = lax.optimization_barrier((part, *down))
     grad_resp = total_of([column[:BLOCK]] + down)
 
-    part = total_of(part).astype(BF16)
-    ring = [part] + [around_x(part, k) for k in (1, 2, 3)]
-    part = total_of([ring[0], ring[2], ring[1], ring[3]]).astype(BF16)
-    part = total_of([part, swap_zl(part, 1)]).astype(BF16)
-    grad_prompt = total_of([part, swap_zl(part, 2)])
+    pieces = gather(total_of(part).astype(BF16), RESP, 16).reshape(4, 4, PIECE, WIDE)
+    grad_prompt = total_of([pieces[:, x] for x in range(4)]).reshape(4 * PIECE, WIDE)
     return (
         out[None],
         dq[None],

time: 143 us -> 133 us (0.930)
  the two profiles are of different devices: /device:TPU:46 before, /device:TPU:8 now
where the time goes in v3:
time: 133 us; the launch traced here: 132 us
  starting transfers between devices  73.6 us (55%)
  waiting for transfers between devices  30.5 us (23%)
  Pallas kernels  17.6 us (13%)
  other arithmetic  4.68 us (4%)
  local copies, waits for them, and re-layouts  3.75 us (3%)
  between operations  1.5 us (1%)
    all_to_all x5, starting transfers between devices, exchange(): return lax.all_to_all(blocks, axes, 0, 0, tiled=True)  41.1 us
    ppermute x6, starting transfers between devices, around_x(): return lax.ppermute(block, 'x', [(x, (x + shift) % 4) for x in range(4)])  21 us
    pallas_call x3, Pallas kernels, call(): pl.pallas_call(kernel, out_shape=tuple((jax.ShapeDtypeStruct(shape, dtype...  17.6 us
    ppermute x6, waiting for transfers between devices, along_zl(): lax.ppermute(block, 'zl', [(z, z + shift) for z in range(4) if 0 <= z + s...  13.2 us
    all_to_all x5, waiting for transfers between devices, exchange(): return lax.all_to_all(blocks, axes, 0, 0, tiled=True)  12.1 us
    ppermute x6, starting transfers between devices, along_zl(): lax.ppermute(block, 'zl', [(z, z + shift) for z in range(4) if 0 <= z + s...  11.5 us
    ppermute x6, waiting for transfers between devices, around_x(): return lax.ppermute(block, 'x', [(x, (x + shift) % 4) for x in range(4)])  5.27 us
  transfers between devices with their start and end apart: 17, of which 10 were waited for; matrix products, arithmetic and copies ran while one was open for 3% of the time, Pallas kernels for 7%

profile of v3, /device:TPU:8, one launch (start us, length us, event | category | flops | bytes accessed | tf_op | source)
XLA Modules:
  0.0 131.7 jit_solution(10961797909696120199)
XLA Ops:
  2.1 15.1 %all-to-all-start = ((bf16[4,64,256]{2,1,0:T(8,128)(2,1)}), bf16[4,64,256]{2,1,0:T(8,128)(2,1)S(1)}, u32[]{:S(2)}, u32[]{:S(2)}) async-start(bf16[4,64,256]{2,1,0:T(8,128)(2,1)} %broadcast_in_dim.32), calls=%async_computation | async-start | bytes 262144 | tf_op jit(solution)/shard_map/all_to_all | solution.py:234
  18.0 3.8 %collective-permute-start.2 = (bf16[128,256]{1,0:T(8,128)(2,1)S(1)}, bf16[128,256]{1,0:T(8,128)(2,1)S(1)}, u32[]{:S(2)}, u32[]{:S(2)}) collective-permute-start(bf16[128,256]{1,0:T(8,128)(2,1)S(1)} %pad_maximum_fusion.1), channel_id=1, source_target_pairs={{0,12},{1,13},{2,14},{3,15},{16,28},{17,29},{18,30},{19,31},{32,44... | collective-permute-start | bytes 196616 | tf_op jit(solution)/shard_map/ppermute | solution.py:246
  21.8 1.3 collective-permute-start.1
  23.1 2.5 %collective-permute-start = (bf16[128,256]{1,0:T(8,128)(2,1)S(1)}, bf16[128,256]{1,0:T(8,128)(2,1)S(1)}, u32[]{:S(2)}, u32[]{:S(2)}) collective-permute-start(bf16[128,256]{1,0:T(8,128)(2,1)S(1)} %pad_maximum_fusion.1), channel_id=1, source_target_pairs={{0,4},{4,8},{8,12},{1,5},{5,9},{9,13},{2,6},{6,10},{10,14},{3,7},{... | collective-permute-start | bytes 196616 | tf_op jit(solution)/shard_map/ppermute | solution.py:246
  26.5 1.6 %collective-permute-done.1 = bf16[128,256]{1,0:T(8,128)(2,1)S(1)} collective-permute-done((bf16[128,256]{1,0:T(8,128)(2,1)S(1)}, bf16[128,256]{1,0:T(8,128)(2,1)S(1)}, u32[]{:S(2)}, u32[]{:S(2)}) %collective-permute-start.1) | collective-permute-done | bytes 65568 | tf_op jit(solution)/shard_map/ppermute | solution.py:246
  29.2 2.5 %all-to-all-done = bf16[4,64,256]{2,1,0:T(8,128)(2,1)S(1)} async-done(((bf16[4,64,256]{2,1,0:T(8,128)(2,1)}), bf16[4,64,256]{2,1,0:T(8,128)(2,1)S(1)}, u32[]{:S(2)}, u32[]{:S(2)}) %all-to-all-start) | async-done | bytes 131104 | tf_op jit(solution)/shard_map/all_to_all | solution.py:234
  32.7 5.0 %all-to-all-start.1 = ((bf16[8,256,256]{2,1,0:T(8,128)(2,1)}), bf16[8,256,256]{2,1,0:T(8,128)(2,1)S(1)}, u32[]{:S(2)}, u32[]{:S(2)}) async-start(bf16[8,256,256]{2,1,0:T(8,128)(2,1)} %broadcast_in_dim.33), calls=%async_computation.1 | async-start | bytes 2097152 | tf_op jit(solution)/shard_map/all_to_all | solution.py:234
  38.6 4.7 %collective-permute-start.5 = (bf16[512,256]{1,0:T(8,128)(2,1)S(1)}, bf16[512,256]{1,0:T(8,128)(2,1)S(1)}, u32[]{:S(2)}, u32[]{:S(2)}) collective-permute-start(bf16[512,256]{1,0:T(8,128)(2,1)S(1)} %pad_maximum_fusion.r0), channel_id=1, source_target_pairs={{0,3},{1,0},{2,1},{3,2},{4,7},{5,4},{6,5},{7,6},{8,11},{9,8},{10,9... | collective-permute-start | bytes 786440 | tf_op jit(solution)/shard_map/ppermute | solution.py:242
  43.9 2.7 %collective-permute-start.4 = (bf16[512,256]{1,0:T(8,128)(2,1)S(1)}, bf16[512,256]{1,0:T(8,128)(2,1)S(1)}, u32[]{:S(2)}, u32[]{:S(2)}) collective-permute-start(bf16[512,256]{1,0:T(8,128)(2,1)S(1)} %pad_maximum_fusion.r0), channel_id=1, source_target_pairs={{0,2},{1,3},{2,0},{3,1},{4,6},{5,7},{6,4},{7,5},{8,10},{9,11},{10,... | collective-permute-start | bytes 786440 | tf_op jit(solution)/shard_map/ppermute | solution.py:242
  46.6 2.8 %collective-permute-start.3 = (bf16[512,256]{1,0:T(8,128)(2,1)S(1)}, bf16[512,256]{1,0:T(8,128)(2,1)S(1)}, u32[]{:S(2)}, u32[]{:S(2)}) collective-permute-start(bf16[512,256]{1,0:T(8,128)(2,1)S(1)} %pad_maximum_fusion.r0), channel_id=1, source_target_pairs={{0,1},{1,2},{2,3},{3,0},{4,5},{5,6},{6,7},{7,4},{8,9},{9,10},{10,1... | collective-permute-start | bytes 786440 | tf_op jit(solution)/shard_map/ppermute | solution.py:242
  49.5 5.3 %collective-permute-done.5.r3 = bf16[512,256]{1,0:T(8,128)(2,1)S(1)} collective-permute-done((bf16[512,256]{1,0:T(8,128)(2,1)S(1)}, bf16[512,256]{1,0:T(8,128)(2,1)S(1)}, u32[]{:S(2)}, u32[]{:S(2)}) %collective-permute-start.5) | collective-permute-done | bytes 262176 | tf_op jit(solution)/shard_map/ppermute | solution.py:242
  54.8 6.3 %shard_map.118 = (bf16[2048,1024]{1,0:T(8,128)(2,1)S(1)}, f32[8,1024]{1,0:T(8,128)S(1)}, f32[8,1024]{1,0:T(8,128)S(1)}, f32[128,1024]{1,0:T(8,128)S(1)}) custom-call(s32[3]{0:T(128)S(1)} %pad_add_fusion.place, bf16[128,1024]{1,0:T(8,128)(2,1)S(1)} %bitcast.33, bf16[2048,256]{1,0:T(8,128)(2,1)S(1)} %bitcast.30, bf16[512,256]{1,0:T(8,128)(2,1)S(1)} %pad_maximum_fusion.r0, ...), custom_call_target="tpu_custom_call" | custom-call | flops 1610612736 | bytes 6291456 | tf_op jit(solution)/shard_map/pallas_call | solution.py:218
  61.1 8.4 %shard_map.119 = (bf16[128,1024]{1,0:T(8,128)(2,1)}, bf16[2048,256]{1,0:T(8,128)(2,1)}, f32[128,1024]{1,0:T(8,128)S(1)}, bf16[128,1024]{1,0:T(8,128)(2,1)S(1)}, ...) custom-call(s32[3]{0:T(128)S(1)} %pad_add_fusion.place, bf16[128,1024]{1,0:T(8,128)(2,1)S(1)} %bitcast.34, ...), custom_call_target="tpu_custom_call" | custom-call | flops 3221225472 | bytes 6291456 | tf_op jit(solution)/shard_map/pallas_call | solution.py:218
  69.4 4.8 %all-to-all-start.2 = ((bf16[8,256,256]{2,1,0:T(8,128)(2,1)}), bf16[8,256,256]{2,1,0:T(8,128)(2,1)}, u32[]{:S(2)}, u32[]{:S(2)}) async-start(bf16[8,256,256]{2,1,0:T(8,128)(2,1)} %bitcast.14), calls=%async_computation.2 | async-start | bytes 2097152 | tf_op jit(solution)/shard_map/all_to_all | solution.py:234
  74.3 3.0 %shard_map.120 = (bf16[128,1024]{1,0:T(8,128)(2,1)}, bf16[4,512,256]{2,1,0:T(8,128)(2,1)S(1)}) custom-call(s32[3]{0:T(128)S(1)} %pad_add_fusion.place, bf16[128,1024]{1,0:T(8,128)(2,1)S(1)} %bitcast.35, bf16[512,256]{1,0:T(8,128)(2,1)S(1)} %pad_maximum_fusion.r0, bf16[512,256]{1,0:T(8,128)(2,1)S(1)} %collective-permute-done.3.r1, ...), custom_call_target="tpu_custom_call" | custom-call | flops 2684354560 | bytes 6291456 | tf_op jit(solution)/shard_map/pallas_call | solution.py:218
  77.3 1.9 %collective-permute-start.6 = (bf16[512,256]{1,0:T(8,128)(2,1)S(1)}, bf16[512,256]{1,0:T(8,128)(2,1)S(1)}, u32[]{:S(2)}, u32[]{:S(2)}) collective-permute-start(bf16[512,256]{1,0:T(8,128)(2,1)S(1)} %get-tuple-element.50), channel_id=1, source_target_pairs={{0,1},{1,2},{2,3},{3,0},{4,5},{5,6},{6,7},{7,4},{8,9},{9,10},{10,1... | collective-permute-start | bytes 786440 | tf_op jit(solution)/shard_map/ppermute | solution.py:242
  79.2 5.6 %collective-permute-start.8 = (bf16[512,256]{1,0:T(8,128)(2,1)S(1)}, bf16[512,256]{1,0:T(8,128)(2,1)S(1)}, u32[]{:S(2)}, u32[]{:S(2)}) collective-permute-start(bf16[512,256]{1,0:T(8,128)(2,1)S(1)} %get-tuple-element.51), channel_id=1, source_target_pairs={{0,3},{1,0},{2,1},{3,2},{4,7},{5,4},{6,5},{7,6},{8,11},{9,8},{10,9... | collective-permute-start | bytes 786440 | tf_op jit(solution)/shard_map/ppermute | solution.py:242
  84.8 3.4 %collective-permute-start.7 = (bf16[512,256]{1,0:T(8,128)(2,1)S(1)}, bf16[512,256]{1,0:T(8,128)(2,1)S(1)}, u32[]{:S(2)}, u32[]{:S(2)}) collective-permute-start(bf16[512,256]{1,0:T(8,128)(2,1)S(1)} %get-tuple-element.52), channel_id=1, source_target_pairs={{0,2},{1,3},{2,0},{3,1},{4,6},{5,7},{6,4},{7,5},{8,10},{9,11},{10,... | collective-permute-start | bytes 786440 | tf_op jit(solution)/shard_map/ppermute | solution.py:242
  88.9 2.0 %convert_reduce_fusion = bf16[256,256]{1,0:T(8,128)(2,1)} fusion(bf16[8,256,256]{2,1,0:T(8,128)(2,1)} %all-to-all-done.2), kind=kLoop, calls=%fused_computation | loop fusion | flops 983040 | bytes 1179648 | tf_op jit(solution)/shard_map/reduce_sum | solution.py:302
  90.9 11.2 %all-to-all-start.3 = ((bf16[16,16,256]{2,1,0:T(8,128)(2,1)}), bf16[16,16,256]{2,1,0:T(8,128)(2,1)S(1)}, u32[]{:S(2)}, u32[]{:S(2)}) async-start(bf16[16,16,256]{2,1,0:T(8,128)(2,1)} %bitcast.15), calls=%async_computation.3 | async-start | bytes 262144 | tf_op jit(solution)/shard_map/all_to_all | solution.py:234
  106.2 7.6 %collective-permute-done.11 = bf16[128,256]{1,0:T(8,128)(2,1)S(1)} collective-permute-done((bf16[128,256]{1,0:T(8,128)(2,1)S(1)}, bf16[128,256]{1,0:T(8,128)(2,1)S(1)}, u32[]{:S(2)}, u32[]{:S(2)}) %collective-permute-start.11) | collective-permute-done | bytes 65568 | tf_op jit(solution)/shard_map/ppermute | solution.py:246
  113.8 2.0 %collective-permute-done.10 = bf16[128,256]{1,0:T(8,128)(2,1)S(1)} collective-permute-done((bf16[128,256]{1,0:T(8,128)(2,1)S(1)}, bf16[128,256]{1,0:T(8,128)(2,1)S(1)}, u32[]{:S(2)}, u32[]{:S(2)}) %collective-permute-start.10) | collective-permute-done | bytes 65568 | tf_op jit(solution)/shard_map/ppermute | solution.py:246
  117.1 5.0 %all-to-all-start.4 = ((bf16[16,16,256]{2,1,0:T(8,128)(2,1)}), bf16[16,16,256]{2,1,0:T(8,128)(2,1)S(1)}, u32[]{:S(2)}, u32[]{:S(2)}) async-start(bf16[16,16,256]{2,1,0:T(8,128)(2,1)} %broadcast_in_dim.39), calls=%async_computation.4 | async-start | bytes 262144 | tf_op jit(solution)/shard_map/all_to_all | solution.py:234
  122.9 8.2 %all-to-all-done.4 = bf16[16,16,256]{2,1,0:T(8,128)(2,1)S(1)} async-done(((bf16[16,16,256]{2,1,0:T(8,128)(2,1)}), bf16[16,16,256]{2,1,0:T(8,128)(2,1)S(1)}, u32[]{:S(2)}, u32[]{:S(2)}) %all-to-all-start.4) | async-done | bytes 131104 | tf_op jit(solution)/shard_map/all_to_all | solution.py:234
  (33 shorter events, 13.6 us)
Async XLA Ops:
  0.6 54.1 %copy-start.1 = (bf16[1,128,1024]{2,1,0:T(8,128)(2,1)S(1)}, bf16[1,128,1024]{2,1,0:T(8,128)(2,1)}, u32[]{:S(2)}) copy-start(bf16[1,128,1024]{2,1,0:T(8,128)(2,1)} %param.7) | copy-start | bytes 786436
  2.1 29.6 %all-to-all-start = ((bf16[4,64,256]{2,1,0:T(8,128)(2,1)}), bf16[4,64,256]{2,1,0:T(8,128)(2,1)S(1)}, u32[]{:S(2)}, u32[]{:S(2)}) async-start(bf16[4,64,256]{2,1,0:T(8,128)(2,1)} %broadcast_in_dim.32), calls=%async_computation | async-start | bytes 262144 | tf_op jit(solution)/shard_map/all_to_all | solution.py:234
  18.0 8.5 %collective-permute-start.2 = (bf16[128,256]{1,0:T(8,128)(2,1)S(1)}, bf16[128,256]{1,0:T(8,128)(2,1)S(1)}, u32[]{:S(2)}, u32[]{:S(2)}) collective-permute-start(bf16[128,256]{1,0:T(8,128)(2,1)S(1)} %pad_maximum_fusion.1), channel_id=1, source_target_pairs={{0,12},{1,13},{2,14},{3,15},{16,28},{17,29},{18,30},{19,31},{32,44... | collective-permute-start | bytes 196616 | tf_op jit(solution)/shard_map/ppermute | solution.py:246
  21.8 6.3 %collective-permute-start.1 = (bf16[128,256]{1,0:T(8,128)(2,1)S(1)}, bf16[128,256]{1,0:T(8,128)(2,1)S(1)}, u32[]{:S(2)}, u32[]{:S(2)}) collective-permute-start(bf16[128,256]{1,0:T(8,128)(2,1)S(1)} %pad_maximum_fusion.1), channel_id=1, source_target_pairs={{0,8},{4,12},{1,9},{5,13},{2,10},{6,14},{3,11},{7,15},{16,24},{20,... | collective-permute-start | bytes 196616 | tf_op jit(solution)/shard_map/ppermute | solution.py:246
  23.1 6.1 %collective-permute-start = (bf16[128,256]{1,0:T(8,128)(2,1)S(1)}, bf16[128,256]{1,0:T(8,128)(2,1)S(1)}, u32[]{:S(2)}, u32[]{:S(2)}) collective-permute-start(bf16[128,256]{1,0:T(8,128)(2,1)S(1)} %pad_maximum_fusion.1), channel_id=1, source_target_pairs={{0,4},{4,8},{8,12},{1,5},{5,9},{9,13},{2,6},{6,10},{10,14},{3,7},{... | collective-permute-start | bytes 196616 | tf_op jit(solution)/shard_map/ppermute | solution.py:246
  32.7 28.3 %copy-start = (bf16[1,128,1024]{2,1,0:T(8,128)(2,1)S(1)}, bf16[1,128,1024]{2,1,0:T(8,128)(2,1)}, u32[]{:S(2)}) copy-start(bf16[1,128,1024]{2,1,0:T(8,128)(2,1)} %param.12) | copy-start | bytes 786436
  32.7 22.0 %all-to-all-start.1 = ((bf16[8,256,256]{2,1,0:T(8,128)(2,1)}), bf16[8,256,256]{2,1,0:T(8,128)(2,1)S(1)}, u32[]{:S(2)}, u32[]{:S(2)}) async-start(bf16[8,256,256]{2,1,0:T(8,128)(2,1)} %broadcast_in_dim.33), calls=%async_computation.1 | async-start | bytes 2097152 | tf_op jit(solution)/shard_map/all_to_all | solution.py:234
  38.6 16.2 %collective-permute-start.5 = (bf16[512,256]{1,0:T(8,128)(2,1)S(1)}, bf16[512,256]{1,0:T(8,128)(2,1)S(1)}, u32[]{:S(2)}, u32[]{:S(2)}) collective-permute-start(bf16[512,256]{1,0:T(8,128)(2,1)S(1)} %pad_maximum_fusion.r0), channel_id=1, source_target_pairs={{0,3},{1,0},{2,1},{3,2},{4,7},{5,4},{6,5},{7,6},{8,11},{9,8},{10,9... | collective-permute-start | bytes 786440 | tf_op jit(solution)/shard_map/ppermute | solution.py:242
  43.9 17.1 %collective-permute-start.4 = (bf16[512,256]{1,0:T(8,128)(2,1)S(1)}, bf16[512,256]{1,0:T(8,128)(2,1)S(1)}, u32[]{:S(2)}, u32[]{:S(2)}) collective-permute-start(bf16[512,256]{1,0:T(8,128)(2,1)S(1)} %pad_maximum_fusion.r0), channel_id=1, source_target_pairs={{0,2},{1,3},{2,0},{3,1},{4,6},{5,7},{6,4},{7,5},{8,10},{9,11},{10,... | collective-permute-start | bytes 786440 | tf_op jit(solution)/shard_map/ppermute | solution.py:242
  46.6 14.4 %collective-permute-start.3 = (bf16[512,256]{1,0:T(8,128)(2,1)S(1)}, bf16[512,256]{1,0:T(8,128)(2,1)S(1)}, u32[]{:S(2)}, u32[]{:S(2)}) collective-permute-start(bf16[512,256]{1,0:T(8,128)(2,1)S(1)} %pad_maximum_fusion.r0), channel_id=1, source_target_pairs={{0,1},{1,2},{2,3},{3,0},{4,5},{5,6},{6,7},{7,4},{8,9},{9,10},{10,1... | collective-permute-start | bytes 786440 | tf_op jit(solution)/shard_map/ppermute | solution.py:242
  69.4 19.4 %all-to-all-start.2 = ((bf16[8,256,256]{2,1,0:T(8,128)(2,1)}), bf16[8,256,256]{2,1,0:T(8,128)(2,1)}, u32[]{:S(2)}, u32[]{:S(2)}) async-start(bf16[8,256,256]{2,1,0:T(8,128)(2,1)} %bitcast.14), calls=%async_computation.2 | async-start | bytes 2097152 | tf_op jit(solution)/shard_map/all_to_all | solution.py:234
  77.3 24.8 %collective-permute-start.6 = (bf16[512,256]{1,0:T(8,128)(2,1)S(1)}, bf16[512,256]{1,0:T(8,128)(2,1)S(1)}, u32[]{:S(2)}, u32[]{:S(2)}) collective-permute-start(bf16[512,256]{1,0:T(8,128)(2,1)S(1)} %get-tuple-element.50), channel_id=1, source_target_pairs={{0,1},{1,2},{2,3},{3,0},{4,5},{5,6},{6,7},{7,4},{8,9},{9,10},{10,1... | collective-permute-start | bytes 786440 | tf_op jit(solution)/shard_map/ppermute | solution.py:242
  79.2 22.9 %collective-permute-start.8 = (bf16[512,256]{1,0:T(8,128)(2,1)S(1)}, bf16[512,256]{1,0:T(8,128)(2,1)S(1)}, u32[]{:S(2)}, u32[]{:S(2)}) collective-permute-start(bf16[512,256]{1,0:T(8,128)(2,1)S(1)} %get-tuple-element.51), channel_id=1, source_target_pairs={{0,3},{1,0},{2,1},{3,2},{4,7},{5,4},{6,5},{7,6},{8,11},{9,8},{10,9... | collective-permute-start | bytes 786440 | tf_op jit(solution)/shard_map/ppermute | solution.py:242
  84.8 17.3 %collective-permute-start.7 = (bf16[512,256]{1,0:T(8,128)(2,1)S(1)}, bf16[512,256]{1,0:T(8,128)(2,1)S(1)}, u32[]{:S(2)}, u32[]{:S(2)}) collective-permute-start(bf16[512,256]{1,0:T(8,128)(2,1)S(1)} %get-tuple-element.52), channel_id=1, source_target_pairs={{0,2},{1,3},{2,0},{3,1},{4,6},{5,7},{6,4},{7,5},{8,10},{9,11},{10,... | collective-permute-start | bytes 786440 | tf_op jit(solution)/shard_map/ppermute | solution.py:242
  90.9 25.6 %all-to-all-start.3 = ((bf16[16,16,256]{2,1,0:T(8,128)(2,1)}), bf16[16,16,256]{2,1,0:T(8,128)(2,1)S(1)}, u32[]{:S(2)}, u32[]{:S(2)}) async-start(bf16[16,16,256]{2,1,0:T(8,128)(2,1)} %bitcast.15), calls=%async_computation.3 | async-start | bytes 262144 | tf_op jit(solution)/shard_map/all_to_all | solution.py:234
  102.3 11.5 %collective-permute-start.11 = (bf16[128,256]{1,0:T(8,128)(2,1)S(1)}, bf16[128,256]{1,0:T(8,128)(2,1)S(1)}, u32[]{:S(2)}, u32[]{:S(2)}) collective-permute-start(bf16[128,256]{1,0:T(8,128)(2,1)S(1)} %get-tuple-element.53), channel_id=1, source_target_pairs={{12,0},{13,1},{14,2},{15,3},{28,16},{29,17},{30,18},{31,19},{44,32... | collective-permute-start | bytes 196616 | tf_op jit(solution)/shard_map/ppermute | solution.py:246
  103.6 12.2 %collective-permute-start.10 = (bf16[128,256]{1,0:T(8,128)(2,1)S(1)}, bf16[128,256]{1,0:T(8,128)(2,1)S(1)}, u32[]{:S(2)}, u32[]{:S(2)}) collective-permute-start(bf16[128,256]{1,0:T(8,128)(2,1)S(1)} %get-tuple-element.54), channel_id=1, source_target_pairs={{8,0},{12,4},{9,1},{13,5},{10,2},{14,6},{11,3},{15,7},{24,16},{28,... | collective-permute-start | bytes 196616 | tf_op jit(solution)/shard_map/ppermute | solution.py:246
  104.9 10.9 %collective-permute-start.9 = (bf16[128,256]{1,0:T(8,128)(2,1)S(1)}, bf16[128,256]{1,0:T(8,128)(2,1)S(1)}, u32[]{:S(2)}, u32[]{:S(2)}) collective-permute-start(bf16[128,256]{1,0:T(8,128)(2,1)S(1)} %get-tuple-element.55), channel_id=1, source_target_pairs={{4,0},{8,4},{12,8},{5,1},{9,5},{13,9},{6,2},{10,6},{14,10},{7,3},{... | collective-permute-start | bytes 196616 | tf_op jit(solution)/shard_map/ppermute | solution.py:246
  117.1 13.9 %all-to-all-start.4 = ((bf16[16,16,256]{2,1,0:T(8,128)(2,1)}), bf16[16,16,256]{2,1,0:T(8,128)(2,1)S(1)}, u32[]{:S(2)}, u32[]{:S(2)}) async-start(bf16[16,16,256]{2,1,0:T(8,128)(2,1)} %broadcast_in_dim.39), calls=%async_computation.4 | async-start | bytes 262144 | tf_op jit(solution)/shard_map/all_to_all | solution.py:234
